TPU v7x, 512 devices: a whole 4x4x16 slice. The times are simulated.
512 devices in a mesh: docs: 64 (over y, z), heads: 8 (over x, core).
Axes of the slice: x: 4, y: 4, z: 16, core: 2. Of those that a mesh axis runs over, the one named last changes fastest.
Arguments:
- queries: bfloat16 [24576, 8192], P('docs', 'heads'), may hold values from -6 to 6
- own_kv: bfloat16 [24576, 2048], P('docs', 'heads'), may hold values from -6 to 6
- cache: bfloat16 [49152, 2048], P('docs', 'heads'), may hold values from -6 to 6
- doc_lists: int32 [128, 20], replicated, may hold values from 0 to 383, as said below
- doc_counts: int32 [128], replicated, may hold values from 8 to 20, as said below
- dev_pos: int32 [384, 24], P('docs'), may hold values from 0 to 127, as said below
- blend_gain: float32 [8, 256], P('heads'), may hold values from 2 to 51
Outputs:
- att_out: bfloat16 [24576, 8192], P('docs', 'heads')
- returned_kv: bfloat16 [4096, 24, 2048], P('docs', None, 'heads')
- dev_score: float32 [128, 20, 24], P('docs')
Inputs may be any that keep to these rules, and one draw needn't show every extreme that they name: `doc_lists`: document d is held by index d // 6 of docs; the lists of one home's 2 requests together hold at most 1 entry naming a document of any one holder. `doc_counts`: some request uses all 20 entries and some uses 8. `dev_pos`: each document's positions are distinct and rising.
All inputs are finite; a program needn't handle non-finite values.
Results may differ from a plain program's by a relative error of at most 0.0046.
Values may be sent and summed in bfloat16 or wider, within the bound.
A program may use at most 64 MiB of HBM per device.

v0:
```python
import jax
import jax.numpy as jnp
from jax import lax
from jax.sharding import PartitionSpec as P

KVH = 8
REQ_DEV = 2
DOC_DEV = 6


very_low = -1e30


def start_state(head_rows, own, dev_rows):
    width = own.shape[1]
    head_dim = width // 2
    group = head_rows.shape[0] // own.shape[0]
    scores = jnp.dot(
        head_rows, own[:, :head_dim].T, preferred_element_type=jnp.float32
    ) * head_dim ** (-0.5)
    token = jnp.arange(head_rows.shape[0], dtype=jnp.int32) // group
    causal = token[:, None] >= jnp.arange(own.shape[0], dtype=jnp.int32)[None, :]
    maxima = jnp.max(jnp.where(causal, scores, very_low), axis=1)
    weights = jnp.where(causal, jnp.exp(scores - maxima[:, None]), 0.0)
    totals = jnp.sum(weights, axis=1)
    summed = jnp.dot(
        weights.astype(jnp.bfloat16), own[:, head_dim:], preferred_element_type=jnp.float32
    )
    dev_count = dev_rows.shape[0]
    return (
        maxima,
        totals,
        summed,
        jnp.full((dev_count,), very_low, jnp.float32),
        jnp.zeros((dev_count,), jnp.float32),
        jnp.zeros((dev_count, width), jnp.float32),
    )


def slot_step(state, block, slot, head_rows, dev_rows, dev_slot):
    maxima, totals, summed, dev_max, dev_tot, dev_sum = state
    head_dim = head_rows.shape[1]
    scale = head_dim ** (-0.5)
    keys = block[:, :head_dim]
    scores = jnp.dot(head_rows, keys.T, preferred_element_type=jnp.float32) * scale
    new_max = jnp.maximum(maxima, jnp.max(scores, axis=1))
    factor = jnp.exp(maxima - new_max)
    weights = jnp.exp(scores - new_max[:, None])
    totals = totals * factor + jnp.sum(weights, axis=1)
    summed = summed * factor[:, None] + jnp.dot(
        weights.astype(jnp.bfloat16), block[:, head_dim:], preferred_element_type=jnp.float32
    )
    dev_scores = jnp.dot(dev_rows[:, :head_dim], keys.T, preferred_element_type=jnp.float32) * scale
    valid = (dev_slot >= slot)[:, None]
    dev_new = jnp.maximum(dev_max, jnp.max(jnp.where(valid, dev_scores, very_low), axis=1))
    dev_factor = jnp.exp(dev_max - dev_new)
    dev_weights = jnp.where(valid, jnp.exp(dev_scores - dev_new[:, None]), 0.0)
    dev_tot = dev_tot * dev_factor + jnp.sum(dev_weights, axis=1)
    dev_sum = dev_sum * dev_factor[:, None] + jnp.dot(
        dev_weights.astype(jnp.bfloat16), block, preferred_element_type=jnp.float32
    )
    return (new_max, totals, summed, dev_new, dev_tot, dev_sum)


def finish(state, dev_rows, gain, tokens):
    maxima, totals, summed, dev_max, dev_tot, dev_sum = state
    head_out = (summed / totals[:, None]).astype(jnp.bfloat16).reshape(tokens, -1)
    correction = dev_sum / dev_tot[:, None]
    delta = gain[None, :] * correction
    updated = (dev_rows.astype(jnp.float32) + delta).astype(jnp.bfloat16)
    squares = jnp.mean(delta * delta, axis=1)
    return (head_out, updated, squares)


def shards(queries, own_kv, cache, doc_lists, doc_counts, dev_pos, blend_gain):
    width = blend_gain.shape[1]
    head_dim = width // 2
    local_heads = blend_gain.shape[0]
    tokens = own_kv.shape[0] // REQ_DEV
    group = queries.shape[1] // (local_heads * head_dim)
    peers = lax.axis_size("docs")
    myself = lax.axis_index("docs")
    slots = doc_lists.shape[1]
    entries = REQ_DEV * slots
    dev_tok = dev_pos.shape[1]
    doc_len = cache.shape[0] // DOC_DEV
    capacity = (entries + peers - 1) // peers
    combined = doc_lists.reshape(peers, entries)
    owners = combined // DOC_DEV
    local_doc = combined % DOC_DEV
    entry_ids = jnp.arange(entries, dtype=jnp.int32)
    same = owners[:, :, None] == owners[:, None, :]
    earlier = entry_ids[None, :] < entry_ids[:, None]
    ranks = jnp.sum((same & earlier[None]).astype(jnp.int32), axis=2)
    blocks = cache.reshape(DOC_DEV, doc_len, cache.shape[1])
    hits = (owners[:, :, None] == myself) & (
        ranks[:, :, None] == jnp.arange(capacity, dtype=jnp.int32)[None, None, :]
    )
    picked = jnp.sum(jnp.where(hits, local_doc[:, :, None], 0), axis=1)
    filled = jnp.any(hits, axis=1)
    zero_value = jnp.zeros((), jnp.bfloat16)
    send_blocks = jnp.where(filled[:, :, None, None], blocks[picked], zero_value)
    mine_owner = lax.dynamic_index_in_dim(owners, myself, 0, keepdims=False)
    mine_rank = lax.dynamic_index_in_dim(ranks, myself, 0, keepdims=False)
    slot_key = mine_owner * capacity + mine_rank
    counts = lax.dynamic_slice_in_dim(doc_counts, myself * REQ_DEV, REQ_DEV, 0)
    dev_blocks = jnp.take_along_axis(blocks, dev_pos[:, :, None], axis=1)
    send_dev = jnp.where(filled[:, :, None, None], dev_blocks[picked], zero_value)
    got_blocks, got_dev = (
        lax.all_to_all(send_blocks, "docs", split_axis=0, concat_axis=0, tiled=True),
        lax.all_to_all(send_dev, "docs", split_axis=0, concat_axis=0, tiled=True),
    )
    context = got_blocks.reshape(peers * capacity, doc_len, cache.shape[1])[slot_key]
    context_dev = got_dev.reshape(peers * capacity, dev_tok, cache.shape[1])[slot_key]
    dev_slot = jnp.arange(slots * dev_tok, dtype=jnp.int32) // dev_tok
    request_outs = []
    request_updates = []
    request_totals = []
    for request in range(REQ_DEV):
        count = counts[request]
        rows_low = request * tokens
        query_rows = queries[rows_low : rows_low + tokens]
        own_rows = own_kv[rows_low : rows_low + tokens]
        request_context = context[request * slots : (request + 1) * slots]
        request_dev = context_dev[request * slots : (request + 1) * slots]
        head_rows = query_rows.reshape(tokens * group, head_dim)
        context_head = request_context
        dev_head = request_dev.reshape(slots * dev_tok, width)
        state = start_state(head_rows, own_rows, dev_head)

        def advance(slot, carry):
            block = lax.dynamic_index_in_dim(context_head, slot, 0, keepdims=False)
            return slot_step(carry, block, slot, head_rows, dev_head, dev_slot)

        state = lax.fori_loop(0, count, advance, state)
        head_out, updated, squares = finish(state, dev_head, blend_gain[0], tokens)
        request_outs.append(head_out)
        request_updates.append(updated.reshape(slots, dev_tok, local_heads * width))
        request_totals.append(squares)
    summed_scores = lax.psum(jnp.stack(request_totals), "heads") / KVH
    live = jnp.arange(slots, dtype=jnp.int32)[None, :] < counts[:, None]
    dev_score = jnp.where(live[:, :, None], summed_scores.reshape(REQ_DEV, slots, dev_tok), 0.0)
    updated_all = jnp.stack(request_updates).reshape(entries, dev_tok, local_heads * width)
    live_flat = live.reshape(entries)
    outgoing = jnp.zeros((peers * capacity, dev_tok, local_heads * width), jnp.bfloat16)
    outgoing = outgoing.at[slot_key].set(
        jnp.where(live_flat[:, None, None], updated_all, zero_value)
    )
    arrived = lax.all_to_all(
        outgoing.reshape(peers, capacity, dev_tok, local_heads * width),
        "docs",
        split_axis=0,
        concat_axis=0,
        tiled=True,
    )
    returned_kv = arrived.reshape(peers * capacity, dev_tok, local_heads * width)
    return (jnp.concatenate(request_outs, axis=0), returned_kv, dev_score)


def solution(mesh):
    return jax.shard_map(
        shards,
        mesh=mesh,
        in_specs=(
            P("docs", "heads"),
            P("docs", "heads"),
            P("docs", "heads"),
            P(),
            P(),
            P("docs", None),
            P("heads", None),
        ),
        out_specs=(P("docs", "heads"), P("docs", None, "heads"), P("docs", None, None)),
        check_vma=False,
    )
```

profile of v0, /device:TPU:6, one launch (start us, length us, event | category | flops | bytes accessed | tf_op | source)
XLA Modules:
  0.0 495.0 jit_solution(5804423369719712066)
XLA Ops:
  4.7 2.3 gather_fusion.4
  8.8 18.7 %all-to-all-start.1 = ((bf16[64,1,24,256]{3,2,1,0:T(8,128)(2,1)}), bf16[64,1,24,256]{3,2,1,0:T(8,128)(2,1)S(1)}, u32[]{:S(2)}, u32[]{:S(2)}) async-start(bf16[64,1,24,256]{3,2,1,0:T(8,128)(2,1)} %bitcast_select_fusion.1), calls=%async_computation.1 | async-start | bytes 1572864 | tf_op jit(solution)/shard_map/all_to_all | solution.py:111
  27.6 2.8 gather_fusion
  30.4 4.5 fusion.42
  34.9 35.6 %all-to-all-done.1 = bf16[64,1,24,256]{3,2,1,0:T(8,128)(2,1)S(1)} async-done(((bf16[64,1,24,256]{3,2,1,0:T(8,128)(2,1)}), bf16[64,1,24,256]{3,2,1,0:T(8,128)(2,1)S(1)}, u32[]{:S(2)}, u32[]{:S(2)}) %all-to-all-start.1) | async-done | bytes 786464 | tf_op jit(solution)/shard_map/all_to_all | solution.py:111
  71.3 6.8 %all-to-all-start = ((bf16[64,1,128,256]{3,2,1,0:T(8,128)(2,1)}), bf16[64,1,128,256]{3,2,1,0:T(8,128)(2,1)}, u32[]{:S(2)}, u32[]{:S(2)}) async-start(bf16[64,1,128,256]{3,2,1,0:T(8,128)(2,1)} %fusion.42), calls=%async_computation | async-start | bytes 8388608 | tf_op jit(solution)/shard_map/all_to_all | solution.py:110
  82.0 1.7 gather_fusion.3
  84.4 181.3 %all-to-all-done = bf16[64,1,128,256]{3,2,1,0:T(8,128)(2,1)} async-done(((bf16[64,1,128,256]{3,2,1,0:T(8,128)(2,1)}), bf16[64,1,128,256]{3,2,1,0:T(8,128)(2,1)}, u32[]{:S(2)}, u32[]{:S(2)}) %all-to-all-start) | async-done | bytes 4194336 | tf_op jit(solution)/shard_map/all_to_all | solution.py:110
  265.8 4.6 gather_fusion.1
  270.4 3.5 fusion.77
  273.9 72.7 %while.42 = (s32[]{:T(128)}, f32[1536]{0:T(1024)S(1)}, f32[1536]{0:T(1024)S(1)}, f32[1536,128]{1,0:T(8,128)S(1)}, f32[480]{0:T(512)S(1)}, /*index=5*/f32[480]{0:...) while((s32[]{:T(128)}, f32[1536]{0:T(1024)S(1)}, ...), condition=%wide.region_12.13_spmd.clone, body=%wide.region_7.12_spmd.clone.sunk | while | flops 150229152 | bytes 6598735 | solution.py:135
  347.4 49.4 %while.43 = (s32[]{:T(128)}, f32[1536]{0:T(1024)S(1)}, f32[1536]{0:T(1024)S(1)}, f32[1536,128]{1,0:T(8,128)S(1)}, f32[480]{0:T(512)S(1)}, /*index=5*/f32[480]{0:...) while((s32[]{:T(128)}, f32[1536]{0:T(1024)S(1)}, ...), condition=%wide.region_20.21_spmd.clone, body=%wide.region_15.20_spmd.clone.sunk | while | flops 150229152 | bytes 6598735 | solution.py:135
  349.1 1.2 select_reduce_fusion.7
  353.5 1.2 select_reduce_fusion.7
  357.9 1.2 select_reduce_fusion.7
  366.8 1.2 select_reduce_fusion.7
  375.6 1.2 select_reduce_fusion.7
  384.5 1.2 select_reduce_fusion.7
  393.3 1.2 select_reduce_fusion.7
  396.9 1.4 multiply_reduce_fusion.1
  399.5 6.2 %scatter_fusion = bf16[64,24,256]{2,1,0:T(8,128)(2,1)} fusion(bf16[64,24,256]{2,1,0:T(8,128)(2,1)} %broadcast_in_dim.149, s32[40]{0:T(128)S(1)} %fusion.70, bf16[40,24,256]{2,1,0:T(8,128)(2,1)S(1)} %bitcast_select_fusion.2), kind=kCustom, calls=%fused_computation.5 | custom fusion | bytes 1474720 | tf_op jit(solution)/shard_map/scatter | solution.py:146
  405.7 45.6 %all-to-all-start.2 = ((bf16[64,1,24,256]{3,2,1,0:T(8,128)(2,1)}), bf16[64,1,24,256]{3,2,1,0:T(8,128)(2,1)S(1)}, u32[]{:S(2)}, u32[]{:S(2)}) async-start(bf16[64,1,24,256]{3,2,1,0:T(8,128)(2,1)} %bitcast.19), calls=%async_computation.2 | async-start | bytes 1572864 | tf_op jit(solution)/shard_map/all_to_all | solution.py:149
  451.3 10.8 %psum.7 = f32[2,480]{1,0:T(2,128)S(1)} all-reduce(f32[2,480]{1,0:T(2,128)S(1)} %pad_maximum_fusion.2), channel_id=1, replica_groups=mesh['docs'=64,'heads'=8] {'heads'}, use_global_device_ids=true, to_apply=%region_24.25 | all-reduce | flops 960 | bytes 7680 | tf_op jit(solution)/shard_map/psum | solution.py:140
  464.7 29.5 %all-to-all-done.2 = bf16[64,1,24,256]{3,2,1,0:T(8,128)(2,1)S(1)} async-done(((bf16[64,1,24,256]{3,2,1,0:T(8,128)(2,1)}), bf16[64,1,24,256]{3,2,1,0:T(8,128)(2,1)S(1)}, u32[]{:S(2)}, u32[]{:S(2)}) %all-to-all-start.2) | async-done | bytes 786464 | tf_op jit(solution)/shard_map/all_to_all | solution.py:149
  (506 shorter events, 107.1 us)
Async XLA Ops:
  0.6 4.1 copy-start
  8.8 61.6 %all-to-all-start.1 = ((bf16[64,1,24,256]{3,2,1,0:T(8,128)(2,1)}), bf16[64,1,24,256]{3,2,1,0:T(8,128)(2,1)S(1)}, u32[]{:S(2)}, u32[]{:S(2)}) async-start(bf16[64,1,24,256]{3,2,1,0:T(8,128)(2,1)} %bitcast_select_fusion.1), calls=%async_computation.1 | async-start | bytes 1572864 | tf_op jit(solution)/shard_map/all_to_all | solution.py:111
  34.9 43.3 %copy-start.3 = (bf16[384,1024]{1,0:T(8,128)(2,1)S(1)}, bf16[384,1024]{1,0:T(8,128)(2,1)}, u32[]{:S(2)}) copy-start(bf16[384,1024]{1,0:T(8,128)(2,1)} %param.11) | copy-start | bytes 2359300
  70.5 0.9 copy-start.2
  71.3 194.4 %all-to-all-start = ((bf16[64,1,128,256]{3,2,1,0:T(8,128)(2,1)}), bf16[64,1,128,256]{3,2,1,0:T(8,128)(2,1)}, u32[]{:S(2)}, u32[]{:S(2)}) async-start(bf16[64,1,128,256]{3,2,1,0:T(8,128)(2,1)} %fusion.42), calls=%async_computation | async-start | bytes 8388608 | tf_op jit(solution)/shard_map/all_to_all | solution.py:110
  78.2 0.7 copy-start.6
  78.2 1.7 copy-start.4
  346.7 0.7 copy-start.1
  347.4 49.5 %copy-start.5 = (f32[1,256]{1,0:T(1,128)S(1)}, f32[1,256]{1,0:T(1,128)}, u32[]{:S(2)}) copy-start(f32[1,256]{1,0:T(1,128)} %param.17) | copy-start | bytes 3076
  405.7 88.5 %all-to-all-start.2 = ((bf16[64,1,24,256]{3,2,1,0:T(8,128)(2,1)}), bf16[64,1,24,256]{3,2,1,0:T(8,128)(2,1)S(1)}, u32[]{:S(2)}, u32[]{:S(2)}) async-start(bf16[64,1,24,256]{3,2,1,0:T(8,128)(2,1)} %bitcast.19), calls=%async_computation.2 | async-start | bytes 1572864 | tf_op jit(solution)/shard_map/all_to_all | solution.py:149
where the time goes:
time: 498 us; the launch traced here: 495 us
  waiting for transfers between devices  246 us (49%)
  starting transfers between devices  71.1 us (14%)
  matrix products  59.5 us (12%)
  local copies, waits for them, and re-layouts  56.6 us (11%)
  other arithmetic  26.6 us (5%)
  loops' own time  23.1 us (5%)
  blocking collectives  10.8 us (2%)
    all_to_all x1, waiting for transfers between devices, shards(): lax.all_to_all(send_blocks, 'docs', split_axis=0, concat_axis=0, tiled=True)  181 us
    all_to_all x1, starting transfers between devices, shards(): lax.all_to_all(outgoing.reshape(peers, capacity, dev_tok, local_heads * w...  45.6 us
    all_to_all x1, waiting for transfers between devices, shards(): lax.all_to_all(send_dev, 'docs', split_axis=0, concat_axis=0, tiled=True)  35.6 us
    all_to_all x1, waiting for transfers between devices, shards(): lax.all_to_all(outgoing.reshape(peers, capacity, dev_tok, local_heads * w...  29.5 us
    squeeze x31, local copies, waits for them, and re-layouts, advance(): block = lax.dynamic_index_in_dim(context_head, slot, 0, keepdims=False)  26.3 us
    another operation x2, loops' own time, shards(): state = lax.fori_loop(0, count, advance, state)  23.1 us
    dot_general x31, matrix products, slot_step(): jnp.dot(dev_rows[:, :head_dim], keys.T, preferred_element_type=jnp.float32)  19.7 us
    dot_general x31, matrix products, slot_step(): jnp.dot(weights.astype(jnp.bfloat16), block[:, head_dim:], preferred_elem...  19 us
  transfers between devices with their start and end apart: 3, of which 3 were waited for; matrix products, arithmetic and copies ran while one was open for 3% of the time, Pallas kernels for 0%

commit v1 on v0

v1 whole, which is shorter than its diff:
```python
import functools

import jax
import jax.numpy as jnp
from jax import lax
from jax.experimental import pallas as pl
from jax.experimental.pallas import tpu as pltpu
from jax.sharding import PartitionSpec as P

KVH = 8
REQ_DEV = 2
DOC_DEV = 6
NZ = 16
very_low = -1e30
VMEM = pltpu.VMEM
SMEM = pltpu.SMEM
LOG2E = 1.4426950408889634
GROUPS = 4


def whole(space):
    return pl.BlockSpec(memory_space=space)


def place(ny, y, z):
    return lax.rem(y + 2 * ny, ny) * NZ + lax.rem(z + 2 * NZ, NZ)


def gather_kernel(ny, sel_ref, cache_ref, ctx_ref, *scratch):
    half = NZ // 2
    full = half - 1
    plus = scratch[:full]
    minus = scratch[full : 2 * full]
    far, picked, zsend, zrecv, ysend, yrecv, local_sem = scratch[2 * full :]
    me = lax.axis_index("docs")
    y, z = me // NZ, lax.rem(me, NZ)
    part = DOC_DEV // 2

    barrier = pltpu.get_barrier_semaphore()
    partners = [place(ny, y, z + 1), place(ny, y, z - 1)]
    partners += [place(ny, y + t, z) for t in range(1, ny)]
    for partner in partners:
        pl.semaphore_signal(barrier, inc=1, device_id={"docs": partner}, device_id_type=pl.DeviceIdType.MESH)
    pl.semaphore_wait(barrier, len(partners))

    def ring(way, step, chunk):
        bufs = plus if way == 0 else minus
        src = cache_ref if step == 1 else bufs[step - 2]
        dst = far if step == half else bufs[step - 1]
        rows = pl.ds(chunk * part, part)
        return pltpu.make_async_remote_copy(
            src_ref=src.at[rows],
            dst_ref=dst.at[rows],
            send_sem=zsend.at[way, step - 1, chunk],
            recv_sem=zrecv.at[way, step - 1, chunk],
            device_id={"docs": partners[way]},
            device_id_type=pl.DeviceIdType.MESH,
        )

    def across(t, j):
        return pltpu.make_async_remote_copy(
            src_ref=picked.at[t, j],
            dst_ref=ctx_ref.at[t * NZ + j],
            send_sem=ysend.at[t, j],
            recv_sem=yrecv.at[t, j],
            device_id={"docs": place(ny, y + t, z)},
            device_id_type=pl.DeviceIdType.MESH,
        )

    def keep(j):
        return pltpu.make_async_copy(picked.at[0, j], ctx_ref.at[j], local_sem.at[j])

    def pick(buf, j):
        for t in list(range(1, ny)) + [0]:
            picked[t, j] = buf[sel_ref[t * NZ + j]]
            if t:
                across(t, j).start()
            else:
                keep(j).start()

    for chunk in range(2):
        for way in range(2):
            ring(way, 1, chunk).start()
    pick(cache_ref, 0)
    for step in range(1, half):
        for chunk in range(2):
            for way in range(2):
                ring(way, step, chunk).wait_recv()
                if step < full or chunk == way:
                    ring(way, step + 1, chunk).start()
        pick(plus[step - 1], step)
        pick(minus[step - 1], NZ - step)
    for way in range(2):
        ring(way, half, way).wait_recv()
    pick(far, half)
    for way in range(2):
        for step in range(1, half + 1):
            for chunk in range(2):
                if step < half or chunk == way:
                    ring(way, step, chunk).wait_send()
    for j in range(NZ):
        for t in range(1, ny):
            across(t, j).wait()
        keep(j).wait()


def gather_docs(sel, cache):
    peers = lax.axis_size("docs")
    ny = peers // NZ
    full = NZ // 2 - 1
    block = cache.shape
    one = block[1:]
    return pl.pallas_call(
        functools.partial(gather_kernel, ny),
        out_shape=jax.ShapeDtypeStruct((peers,) + one, cache.dtype),
        in_specs=[whole(SMEM), whole(VMEM)],
        out_specs=whole(pl.ANY),
        scratch_shapes=[VMEM(block, cache.dtype)] * (2 * full + 1)
        + [
            VMEM((ny, NZ) + one, cache.dtype),
            pltpu.SemaphoreType.DMA((2, NZ // 2, 2)),
            pltpu.SemaphoreType.DMA((2, NZ // 2, 2)),
            pltpu.SemaphoreType.DMA((ny, NZ)),
            pltpu.SemaphoreType.DMA((ny, NZ)),
            pltpu.SemaphoreType.DMA((NZ,)),
        ],
        compiler_params=pltpu.CompilerParams(
            collective_id=0, has_side_effects=True, vmem_limit_bytes=24 * 2**20
        ),
        cost_estimate=pl.CostEstimate(flops=0, bytes_accessed=200 * 10**6, transcendentals=0),
        name="gather_docs",
    )(sel, cache)


def dev_kernel(slots, slot_ref, count_ref, ctx_ref, pos_ref, gain_ref, upd_ref, sq_ref, kv, dev, sems):
    entries = REQ_DEV * slots
    doc_len, width = ctx_ref.shape[1:]
    head_dim = width // 2
    dev_tok = pos_ref.shape[0] // entries
    group = slots // GROUPS
    scale = head_dim ** (-0.5)

    def bring(e):
        return pltpu.make_async_copy(
            ctx_ref.at[slot_ref[e]], kv.at[pl.ds(e * doc_len, doc_len)], sems.at[e]
        )

    for e in range(entries):
        bring(e).start()
    upd_ref[...] = jnp.zeros_like(upd_ref)
    token = lax.broadcasted_iota(jnp.int32, (dev_tok, doc_len), 1)
    for r in range(REQ_DEV):
        count = count_ref[r]
        base = r * slots * doc_len
        for e in range(r * slots, (r + 1) * slots):
            bring(e).wait()
        for e in range(r * slots, (r + 1) * slots):
            hot = (pos_ref[e * dev_tok : (e + 1) * dev_tok] == token).astype(jnp.bfloat16)
            dev[e * dev_tok : (e + 1) * dev_tok] = jnp.dot(
                hot, kv[e * doc_len : (e + 1) * doc_len], preferred_element_type=jnp.float32
            )
        for g in range(GROUPS):
            first = r * slots + g * group
            rows = slice(first * dev_tok, (first + group) * dev_tok)
            tokens = (g + 1) * group * doc_len

            @pl.when(g * group < count)
            def _():
                mine = dev[rows]
                keys = kv[base : base + tokens, :head_dim]
                scores = lax.dot_general(
                    mine[:, :head_dim].astype(jnp.bfloat16),
                    keys,
                    (((1,), (1,)), ((), ())),
                    preferred_element_type=jnp.float32,
                )
                row_slot = lax.broadcasted_iota(jnp.int32, scores.shape, 0) // dev_tok + g * group
                key_slot = lax.broadcasted_iota(jnp.int32, scores.shape, 1) // doc_len
                scores = jnp.where(row_slot >= key_slot, scores, very_low)
                top = jnp.max(scores, axis=1, keepdims=True)
                weights = jnp.exp2((scores - top) * (scale * LOG2E))
                total = jnp.sum(weights, axis=1, keepdims=True)
                summed = jnp.dot(
                    weights.astype(jnp.bfloat16),
                    kv[base : base + tokens],
                    preferred_element_type=jnp.float32,
                )
                delta = gain_ref[...] * (summed / total)
                fresh = mine + delta
                square = jnp.sum(delta * delta, axis=1, keepdims=True) * (1.0 / width)
                sq_ref[rows] = jnp.broadcast_to(square, (group * dev_tok, 128))
                for i in range(group):

                    @pl.when(g * group + i < count)
                    def _():
                        one = fresh[i * dev_tok : (i + 1) * dev_tok]
                        upd_ref[slot_ref[first + i]] = jnp.concatenate(
                            [one[:, :head_dim], one[:, head_dim:]], axis=0
                        ).astype(jnp.bfloat16)

            @pl.when(g * group >= count)
            def _():
                sq_ref[rows] = jnp.zeros((group * dev_tok, 128), jnp.float32)


def deviations(slots, slot_of, counts, ctx, pos, gain):
    entries = REQ_DEV * slots
    peers, doc_len, width = ctx.shape
    dev_tok = pos.shape[0] // entries
    return pl.pallas_call(
        functools.partial(dev_kernel, slots),
        out_shape=(
            jax.ShapeDtypeStruct((peers, 2 * dev_tok, width // 2), jnp.bfloat16),
            jax.ShapeDtypeStruct((entries * dev_tok, 128), jnp.float32),
        ),
        in_specs=[whole(SMEM), whole(SMEM), whole(pl.ANY), whole(VMEM), whole(VMEM)],
        out_specs=(whole(VMEM), whole(VMEM)),
        scratch_shapes=[
            VMEM((entries * doc_len, width), jnp.bfloat16),
            VMEM((entries * dev_tok, width), jnp.float32),
            pltpu.SemaphoreType.DMA((entries,)),
        ],
        compiler_params=pltpu.CompilerParams(vmem_limit_bytes=40 * 2**20),
        cost_estimate=pl.CostEstimate(
            flops=2 * 2 * 480 * 2560 * 384, bytes_accessed=5 * 10**6, transcendentals=2 * 10**6
        ),
        name="deviations",
    )(slot_of, counts, ctx, pos, gain)


def attend_kernel(
    ny, slots, slot_ref, count_ref, ctx_ref, upd_ref, q_ref, own_ref, att_ref, ret_ref, ctx, kv, send, recv, local_sem
):
    peers, doc_len, width = ctx_ref.shape
    head_dim = width // 2
    tokens = own_ref.shape[0] // REQ_DEV
    group = q_ref.shape[1] // head_dim
    span = kv.shape[0]
    scale = head_dim ** (-0.5)
    me = lax.axis_index("docs")
    y, z = me // NZ, lax.rem(me, NZ)

    stage = pltpu.make_async_copy(ctx_ref, ctx, local_sem.at[0])
    stage.start()
    barrier = pltpu.get_barrier_semaphore()

    def greet(s, carry):
        pl.semaphore_signal(
            barrier,
            inc=1,
            device_id={"docs": place(ny, y - s // NZ, z - lax.rem(s, NZ))},
            device_id_type=pl.DeviceIdType.MESH,
        )
        return carry

    lax.fori_loop(1, peers, greet, 0)
    pl.semaphore_wait(barrier, peers - 1)

    def back(s):
        return pltpu.make_async_remote_copy(
            src_ref=upd_ref.at[s],
            dst_ref=ret_ref.at[me],
            send_sem=send.at[s],
            recv_sem=recv.at[s],
            device_id={"docs": place(ny, y - s // NZ, z - lax.rem(s, NZ))},
            device_id_type=pl.DeviceIdType.MESH,
        )

    def launch(i, carry):
        back(i).start()
        return carry

    lax.fori_loop(1, peers, launch, 0)
    mine = pltpu.make_async_copy(upd_ref.at[0], ret_ref.at[me], local_sem.at[1])
    mine.start()

    row = lax.broadcasted_iota(jnp.int32, (tokens, span - slots * doc_len), 0)
    col = lax.broadcasted_iota(jnp.int32, (tokens, span - slots * doc_len), 1)
    causal = row >= col
    used = lax.broadcasted_iota(jnp.int32, (1, slots * doc_len), 1)
    kv[slots * doc_len :] = jnp.zeros((span - slots * doc_len, width), kv.dtype)
    stage.wait()
    for r in range(REQ_DEV):
        count = count_ref[r]

        def load(k, carry):
            kv[pl.ds(pl.multiple_of(k * doc_len, doc_len), doc_len)] = ctx[slot_ref[r * slots + k]]
            return carry

        lax.fori_loop(0, slots, load, 0)
        kv[slots * doc_len : slots * doc_len + tokens] = own_ref[r * tokens : (r + 1) * tokens]
        live = used < count * doc_len

        def head(i, carry):
            cols = pl.ds(pl.multiple_of(i * head_dim, head_dim), head_dim)
            scores = lax.dot_general(
                q_ref[r * tokens : (r + 1) * tokens, cols],
                kv[:, :head_dim],
                (((1,), (1,)), ((), ())),
                preferred_element_type=jnp.float32,
            )
            docs = jnp.where(live, scores[:, : slots * doc_len], very_low)
            self = jnp.where(causal, scores[:, slots * doc_len :], very_low)
            top = jnp.maximum(
                jnp.max(docs, axis=1, keepdims=True), jnp.max(self, axis=1, keepdims=True)
            )
            docs = jnp.exp2((docs - top) * (scale * LOG2E))
            self = jnp.exp2((self - top) * (scale * LOG2E))
            total = jnp.sum(docs, axis=1, keepdims=True) + jnp.sum(self, axis=1, keepdims=True)
            summed = jnp.dot(
                docs.astype(jnp.bfloat16),
                kv[: slots * doc_len, head_dim:],
                preferred_element_type=jnp.float32,
            ) + jnp.dot(
                self.astype(jnp.bfloat16),
                kv[slots * doc_len :, head_dim:],
                preferred_element_type=jnp.float32,
            )
            att_ref[r * tokens : (r + 1) * tokens, cols] = (summed / total).astype(jnp.bfloat16)
            return carry

        lax.fori_loop(0, group, head, 0)

    def land(i, carry):
        back(i).wait()
        return carry

    lax.fori_loop(1, peers, land, 0)
    mine.wait()


def attend_and_return(slots, slot_of, counts, ctx, upd, queries, own):
    peers, doc_len, width = ctx.shape
    ny = peers // NZ
    tokens = own.shape[0] // REQ_DEV
    span = slots * doc_len + (tokens + 127) // 128 * 128
    return pl.pallas_call(
        functools.partial(attend_kernel, ny, slots),
        out_shape=(
            jax.ShapeDtypeStruct(queries.shape, jnp.bfloat16),
            jax.ShapeDtypeStruct(upd.shape, jnp.bfloat16),
        ),
        in_specs=[whole(SMEM), whole(SMEM), whole(pl.ANY), whole(pl.ANY), whole(VMEM), whole(VMEM)],
        out_specs=(whole(VMEM), whole(pl.ANY)),
        scratch_shapes=[
            VMEM(ctx.shape, ctx.dtype),
            VMEM((span, width), ctx.dtype),
            pltpu.SemaphoreType.DMA((peers,)),
            pltpu.SemaphoreType.DMA((peers,)),
            pltpu.SemaphoreType.DMA((2,)),
        ],
        compiler_params=pltpu.CompilerParams(
            collective_id=1, has_side_effects=True, vmem_limit_bytes=40 * 2**20
        ),
        cost_estimate=pl.CostEstimate(
            flops=9 * 10**9, bytes_accessed=100 * 10**6, transcendentals=9 * 10**6
        ),
        name="attend_and_return",
    )(slot_of, counts, ctx, upd, queries, own)


def shards(queries, own_kv, cache, doc_lists, doc_counts, dev_pos, blend_gain):
    width = blend_gain.shape[1]
    head_dim = width // 2
    peers = lax.axis_size("docs")
    ny = peers // NZ
    me = lax.axis_index("docs")
    y, z = me // NZ, me % NZ
    slots = doc_lists.shape[1]
    entries = REQ_DEV * slots
    dev_tok = dev_pos.shape[1]
    doc_len = cache.shape[0] // DOC_DEV
    combined = doc_lists.reshape(peers, entries)

    row_lists = jnp.roll(combined.reshape(ny, NZ, entries)[:, z], -y, axis=0)
    row_owner = row_lists // DOC_DEV
    steps = jnp.arange(NZ, dtype=jnp.int32)
    passing = y * NZ + (z - steps) % NZ
    hits = row_owner[:, :, None] == passing[None, None, :]
    sel = jnp.sum(jnp.where(hits, (row_lists % DOC_DEV)[:, :, None], 0), axis=1).reshape(-1)

    mine = combined[me]
    owner = mine // DOC_DEV
    slot_of = ((y - owner // NZ) % ny) * NZ + (z - owner % NZ) % NZ
    counts = lax.dynamic_slice_in_dim(doc_counts, me * REQ_DEV, REQ_DEV, 0)

    all_pos = lax.all_gather(dev_pos, "docs", axis=0, tiled=True)
    ctx = gather_docs(sel.astype(jnp.int32), cache.reshape(DOC_DEV, doc_len, width))
    pos = jnp.broadcast_to(all_pos[mine].reshape(-1, 1), (entries * dev_tok, doc_len))
    upd, squares = deviations(slots, slot_of, counts, ctx, pos, blend_gain)
    scores = lax.psum(squares[:, 0], "heads") / KVH
    live = jnp.arange(slots, dtype=jnp.int32)[None, :] < counts[:, None]
    dev_score = jnp.where(live[:, :, None], scores.reshape(REQ_DEV, slots, dev_tok), 0.0)
    att, ret = attend_and_return(slots, slot_of, counts, ctx, upd, queries, own_kv)
    returned = jnp.concatenate([ret[:, :dev_tok], ret[:, dev_tok:]], axis=2)
    return att, returned, dev_score


def solution(mesh):
    return jax.shard_map(
        shards,
        mesh=mesh,
        in_specs=(
            P("docs", "heads"),
            P("docs", "heads"),
            P("docs", "heads"),
            P(),
            P(),
            P("docs", None),
            P("heads", None),
        ),
        out_specs=(P("docs", "heads"), P("docs", None, "heads"), P("docs", None, None)),
        check_vma=False,
    )
```

time: 498 us -> 237 us (0.48)
  waiting for transfers between devices: 246 us -> 0 us
  Pallas kernels: 0 us -> 131 us
  blocking collectives: 10.8 us -> 91.2 us
  starting transfers between devices: 71.1 us -> 0 us
  matrix products: 59.5 us -> 0 us
  local copies, waits for them, and re-layouts: 56.6 us -> 9 us
  other arithmetic: 26.6 us -> 1.42 us
  loops' own time: 23.1 us -> 0 us
    all_to_all x3 -> x0, waiting for transfers between devices: 246 us -> none  [the longest x1 181 us: shards(): lax.all_to_all(send_blocks, 'docs', split_axis=0, concat_axis=0, tiled=True)]
    pallas_call x0 -> x3, Pallas kernels: none -> 131 us  [the longest x1 85.2 us: gather_docs(): pl.pallas_call(functools.partial(gather_kernel, ny), out_shape=jax.ShapeD...]
    all_gather x0 -> x1, blocking collectives: none -> 81.2 us  [shards(): all_pos = lax.all_gather(dev_pos, 'docs', axis=0, tiled=True)]
    all_to_all x3 -> x0, starting transfers between devices: 71.1 us -> none  [the longest x1 45.6 us: shards(): lax.all_to_all(outgoing.reshape(peers, capacity, dev_tok, local_heads * w...]
    dot_general x128 -> x0, matrix products: 59.5 us -> none  [the longest x31 19.7 us: slot_step(): jnp.dot(dev_rows[:, :head_dim], keys.T, preferred_element_type=jnp.float32)]
    squeeze x31 -> x0, local copies, waits for them, and re-layouts: 26.3 us -> none  [advance(): block = lax.dynamic_index_in_dim(context_head, slot, 0, keepdims=False)]
    another operation x2 -> x0, loops' own time: 23.1 us -> none  [shards(): state = lax.fori_loop(0, count, advance, state)]
    reduce_sum x67 -> x1, other arithmetic: 15.7 us -> 0.21 us  [shards(): jnp.sum(jnp.where(hits, (row_lists % DOC_DEV)[:, :, None], 0), axis=1)]
  transfers between devices with their start and end apart: 3 -> 0, of which waited for: 3 -> 0; matrix products, arithmetic and copies ran while one was open for 3% -> 0% of each run, Pallas kernels for 0% -> 0%
where the time goes in v1:
time: 237 us; the launch traced here: 233 us
  Pallas kernels  131 us (55%)
  blocking collectives  91.2 us (38%)
  local copies, waits for them, and re-layouts  9 us (4%)
    pallas_call x1, Pallas kernels, gather_docs(): pl.pallas_call(functools.partial(gather_kernel, ny), out_shape=jax.ShapeD...  85.2 us
    all_gather x1, blocking collectives, shards(): all_pos = lax.all_gather(dev_pos, 'docs', axis=0, tiled=True)  81.2 us
    pallas_call x1, Pallas kernels, attend_and_return(): pl.pallas_call(functools.partial(attend_kernel, ny, slots), out_shape=(ja...  34.2 us
    pallas_call x1, Pallas kernels, deviations(): pl.pallas_call(functools.partial(dev_kernel, slots), out_shape=(jax.Shape...  11.4 us
    psum x1, blocking collectives, shards(): scores = lax.psum(squares[:, 0], 'heads') / KVH  10 us
    unnamed x20, local copies, waits for them, and re-layouts  7.47 us

profile of v1, /device:TPU:6, one launch (start us, length us, event | category | flops | bytes accessed | tf_op | source)
XLA Modules:
  0.0 233.2 jit_solution(9118737771402315335)
XLA Ops:
  0.7 0.8 copy.16
  1.5 0.1 reshape_reshape.3
  1.6 0.2 select_reduce_fusion
  1.8 0.1 reshape.98.sel_ref
  1.9 1.0 copy-done.2
  2.9 85.2 %gather_docs.1.ctx_ref = bf16[64,128,256]{2,1,0:T(8,128)(2,1)S(1)} custom-call(s32[64]{0:T(128)S(1)} %reshape.98.sel_ref, bf16[6,128,256]{2,1,0:T(8,128)(2,1)S(1)} %bitcast.15), custom_call_target="tpu_custom_call" | custom-call | bytes 200000000 | tf_op jit(solution)/shard_map/gather_docs/pallas_call | solution.py:113
  88.1 1.9 copy-done
  90.1 0.1 reshape.97
  90.2 0.1 dynamic_slice.14.count_ref
  90.3 81.2 %all-gather = s32[64,6,24]{2,1,0:T(8,128)S(1)} all-gather(s32[1,6,24]{2,1,0:T(8,128)S(1)} %bitcast.17), channel_id=1, replica_groups=mesh['docs'=64,'heads'=8] {'docs'}, dimensions={0}, use_global_device_ids=true | all-gather | bytes 37440 | tf_op jit(solution)/shard_map/all_gather | solution.py:387
  171.5 0.6 gather_fusion
  172.1 0.1 broadcast_in_dim.40
  172.2 0.2 broadcast_in_dim.41.pos_ref
  172.4 2.2 copy-done.1
  174.6 11.4 %deviations.1 = (bf16[64,48,128]{2,1,0:T(8,128)(2,1)S(1)}, f32[960,128]{1,0:T(8,128)S(1)}) custom-call(s32[40]{0:T(128)S(1)} %fusion.1.slot_ref, s32[2]{0:T(128)S(1)} %dynamic_slice.14.count_ref, bf16[64,128,256]{2,1,0:T(8,128)(2,1)S(1)} %copy-done.1, s32[960,128]{1,0:T(8,128)S(1)} %broadcast_in_dim.41.pos_ref, f32[1,256]{1,0:T(1,128)S(1)} %copy-done.5), custom_call_target="tpu_custom_call" | custom-call | flops 1887436800 | bytes 5000000 | tf_op jit(solution)/shard_map/deviations/pallas_call | solution.py:210
  186.0 34.2 %attend_and_return.1 = (bf16[384,1024]{1,0:T(8,128)(2,1)S(1)}, bf16[64,48,128]{2,1,0:T(8,128)(2,1)S(1)}) custom-call(s32[40]{0:T(128)S(1)} %fusion.1.slot_ref, s32[2]{0:T(128)S(1)} %dynamic_slice.14.count_ref, bf16[64,128,256]{2,1,0:T(8,128)(2,1)S(1)} %copy-done.1, bf16[64,48,128]{2,1,0:T(8,128)(2,1)S(1)} %get-tuple-element.7.upd_ref, ...), custom_call_target="tpu_custom_call" | custom-call | flops 8999999488 | bytes 100000000 | tf_op jit(solution)/shard_map/attend_and_return/pallas_call | solution.py:337
  220.2 0.1 fusion.9
  220.2 1.0 pad_maximum_fusion
  221.2 0.2 slice_reduce_fusion
  221.4 10.0 %psum.7 = f32[960]{0:T(1024)S(1)} all-reduce(f32[960]{0:T(1024)S(1)} %slice_reduce_fusion), channel_id=1, replica_groups=mesh['docs'=64,'heads'=8] {'heads'}, use_global_device_ids=true, to_apply=%region_1.2 | all-reduce | flops 960 | bytes 7680 | tf_op jit(solution)/shard_map/psum | solution.py:391
  231.4 0.1 reshape.100
  231.6 0.1 broadcast_select_fusion
  231.7 0.6 copy.18
  232.3 0.9 copy.20
  (23 shorter events, 0.2 us)
Async XLA Ops:
  1.9 1.0 copy-start.2
  2.9 87.2 %copy-start.7 = (s32[128]{0:T(128)S(1)}, s32[128]{0:T(128)}, u32[]{:S(2)}) copy-start(s32[128]{0:T(128)} %param.11) | copy-start | bytes 1540
  2.9 87.3 %copy-start.6 = (s32[6,24]{1,0:T(8,128)S(1)}, s32[6,24]{1,0:T(8,128)}, u32[]{:S(2)}) copy-start(s32[6,24]{1,0:T(8,128)} %param.12) | copy-start | bytes 1732
  2.9 169.4 %copy-start.5 = (f32[1,256]{1,0:T(1,128)S(1)}, f32[1,256]{1,0:T(1,128)}, u32[]{:S(2)}) copy-start(f32[1,256]{1,0:T(1,128)} %gain_ref.1) | copy-start | bytes 3076
  88.1 1.9 copy-start
  172.4 2.2 copy-start.1
  174.5 11.4 %copy-start.3 = (bf16[384,1024]{1,0:T(8,128)(2,1)S(1)}, bf16[384,1024]{1,0:T(8,128)(2,1)}, u32[]{:S(2)}) copy-start(bf16[384,1024]{1,0:T(8,128)(2,1)} %q_ref.1) | copy-start | bytes 2359300
  174.5 11.4 %copy-start.4 = (bf16[384,256]{1,0:T(8,128)(2,1)S(1)}, bf16[384,256]{1,0:T(8,128)(2,1)}, u32[]{:S(2)}) copy-start(bf16[384,256]{1,0:T(8,128)(2,1)} %own_ref.1) | copy-start | bytes 589828

commit v2 on v1

--- a/solution.py
+++ b/solution.py
@@ -16,6 +16,7 @@
 SMEM = pltpu.SMEM
 LOG2E = 1.4426950408889634
 GROUPS = 4
+WINDOW = 3
 
 
 def whole(space):
@@ -26,12 +27,12 @@
     return lax.rem(y + 2 * ny, ny) * NZ + lax.rem(z + 2 * NZ, NZ)
 
 
-def gather_kernel(ny, sel_ref, cache_ref, ctx_ref, *scratch):
+def gather_kernel(ny, sel_ref, cache_ref, pos_ref, ctx_ref, allpos_ref, *scratch):
     half = NZ // 2
     full = half - 1
     plus = scratch[:full]
     minus = scratch[full : 2 * full]
-    far, picked, zsend, zrecv, ysend, yrecv, local_sem = scratch[2 * full :]
+    far, picked, ring_pos, zsend, zrecv, ysend, yrecv, psend, precv, local_sem = scratch[2 * full :]
     me = lax.axis_index("docs")
     y, z = me // NZ, lax.rem(me, NZ)
     part = DOC_DEV // 2
@@ -41,19 +42,43 @@
     partners += [place(ny, y + t, z) for t in range(1, ny)]
     for partner in partners:
         pl.semaphore_signal(barrier, inc=1, device_id={"docs": partner}, device_id_type=pl.DeviceIdType.MESH)
+    ring_pos[0] = pos_ref[...]
     pl.semaphore_wait(barrier, len(partners))
 
-    def ring(way, step, chunk):
+    order = [(step, doc) for step in range(1, half) for doc in range(DOC_DEV)]
+    orders = [order + [(half, way * part + doc) for doc in range(part)] for way in range(2)]
+
+    def ring(way, step, doc):
         bufs = plus if way == 0 else minus
         src = cache_ref if step == 1 else bufs[step - 2]
         dst = far if step == half else bufs[step - 1]
-        rows = pl.ds(chunk * part, part)
         return pltpu.make_async_remote_copy(
-            src_ref=src.at[rows],
-            dst_ref=dst.at[rows],
-            send_sem=zsend.at[way, step - 1, chunk],
-            recv_sem=zrecv.at[way, step - 1, chunk],
+            src_ref=src.at[doc],
+            dst_ref=dst.at[doc],
+            send_sem=zsend.at[way, step - 1, doc],
+            recv_sem=zrecv.at[way, step - 1, doc],
             device_id={"docs": partners[way]},
+            device_id_type=pl.DeviceIdType.MESH,
+        )
+
+    def ring_of_pos(way, step):
+        src, dst = (step - 1, step) if way == 0 else ((NZ - step + 1) % NZ, NZ - step)
+        return pltpu.make_async_remote_copy(
+            src_ref=ring_pos.at[src],
+            dst_ref=ring_pos.at[dst],
+            send_sem=psend.at[way, step],
+            recv_sem=precv.at[way, step],
+            device_id={"docs": partners[way]},
+            device_id_type=pl.DeviceIdType.MESH,
+        )
+
+    def pos_across(t):
+        return pltpu.make_async_remote_copy(
+            src_ref=ring_pos,
+            dst_ref=allpos_ref.at[t],
+            send_sem=psend.at[0, half + t],
+            recv_sem=precv.at[0, half + t],
+            device_id={"docs": place(ny, y + t, z)},
             device_id_type=pl.DeviceIdType.MESH,
         )
 
@@ -70,6 +95,8 @@
     def keep(j):
         return pltpu.make_async_copy(picked.at[0, j], ctx_ref.at[j], local_sem.at[j])
 
+    keep_pos = pltpu.make_async_copy(ring_pos, allpos_ref.at[0], local_sem.at[NZ])
+
     def pick(buf, j):
         for t in list(range(1, ny)) + [0]:
             picked[t, j] = buf[sel_ref[t * NZ + j]]
@@ -78,33 +105,56 @@
             else:
                 keep(j).start()
 
-    for chunk in range(2):
+    for n in range(len(orders[0])):
         for way in range(2):
-            ring(way, 1, chunk).start()
-    pick(cache_ref, 0)
-    for step in range(1, half):
-        for chunk in range(2):
+            step, doc = orders[way][n]
+            if step > 1:
+                ring(way, step - 1, doc).wait_recv()
+            if n >= WINDOW:
+                ring(way, *orders[way][n - WINDOW]).wait_send()
+            ring(way, step, doc).start()
+        step, doc = order[n] if n < len(order) else (half, n - len(order))
+        if doc == 0:
             for way in range(2):
-                ring(way, step, chunk).wait_recv()
-                if step < full or chunk == way:
-                    ring(way, step + 1, chunk).start()
-        pick(plus[step - 1], step)
-        pick(minus[step - 1], NZ - step)
+                if step > 1 and (way == 0 or step <= half):
+                    ring_of_pos(way, step - 1).wait_recv()
+                if way == 0 or step < half:
+                    ring_of_pos(way, step).start()
+        if n == WINDOW - 1:
+            pick(cache_ref, 0)
+        if step > 1 and step < half and doc == DOC_DEV - 1:
+            pick(plus[step - 2], step - 1)
+            pick(minus[step - 2], NZ - step + 1)
     for way in range(2):
-        ring(way, half, way).wait_recv()
+        for doc in range(DOC_DEV):
+            if not part * way <= doc < part * (way + 1):
+                ring(way, full, doc).wait_recv()
+    pick(plus[full - 1], full)
+    pick(minus[full - 1], NZ - full)
+    ring_of_pos(0, half).wait_recv()
+    for t in range(1, ny):
+        pos_across(t).start()
+    keep_pos.start()
+    for way in range(2):
+        for doc in range(part):
+            ring(way, half, way * part + doc).wait_recv()
     pick(far, half)
     for way in range(2):
+        for n in range(len(orders[way]) - WINDOW, len(orders[way])):
+            ring(way, *orders[way][n]).wait_send()
         for step in range(1, half + 1):
-            for chunk in range(2):
-                if step < half or chunk == way:
-                    ring(way, step, chunk).wait_send()
+            if way == 0 or step < half:
+                ring_of_pos(way, step).wait_send()
     for j in range(NZ):
         for t in range(1, ny):
             across(t, j).wait()
         keep(j).wait()
-
-
-def gather_docs(sel, cache):
+    for t in range(1, ny):
+        pos_across(t).wait()
+    keep_pos.wait()
+
+
+def gather_docs(sel, cache, pos):
     peers = lax.axis_size("docs")
     ny = peers // NZ
     full = NZ // 2 - 1
@@ -112,31 +162,36 @@
     one = block[1:]
     return pl.pallas_call(
         functools.partial(gather_kernel, ny),
-        out_shape=jax.ShapeDtypeStruct((peers,) + one, cache.dtype),
-        in_specs=[whole(SMEM), whole(VMEM)],
-        out_specs=whole(pl.ANY),
+        out_shape=(
+            jax.ShapeDtypeStruct((peers,) + one, cache.dtype),
+            jax.ShapeDtypeStruct((ny, NZ) + pos.shape, pos.dtype),
+        ),
+        in_specs=[whole(SMEM), whole(VMEM), whole(VMEM)],
+        out_specs=(whole(pl.ANY), whole(pl.ANY)),
         scratch_shapes=[VMEM(block, cache.dtype)] * (2 * full + 1)
         + [
             VMEM((ny, NZ) + one, cache.dtype),
-            pltpu.SemaphoreType.DMA((2, NZ // 2, 2)),
-            pltpu.SemaphoreType.DMA((2, NZ // 2, 2)),
+            VMEM((NZ,) + pos.shape, pos.dtype),
+            pltpu.SemaphoreType.DMA((2, NZ // 2, DOC_DEV)),
+            pltpu.SemaphoreType.DMA((2, NZ // 2, DOC_DEV)),
             pltpu.SemaphoreType.DMA((ny, NZ)),
             pltpu.SemaphoreType.DMA((ny, NZ)),
-            pltpu.SemaphoreType.DMA((NZ,)),
+            pltpu.SemaphoreType.DMA((2, NZ // 2 + ny)),
+            pltpu.SemaphoreType.DMA((2, NZ // 2 + ny)),
+            pltpu.SemaphoreType.DMA((NZ + 1,)),
         ],
         compiler_params=pltpu.CompilerParams(
             collective_id=0, has_side_effects=True, vmem_limit_bytes=24 * 2**20
         ),
         cost_estimate=pl.CostEstimate(flops=0, bytes_accessed=200 * 10**6, transcendentals=0),
         name="gather_docs",
-    )(sel, cache)
-
-
-def dev_kernel(slots, slot_ref, count_ref, ctx_ref, pos_ref, gain_ref, upd_ref, sq_ref, kv, dev, sems):
+    )(sel, cache, pos)
+
+
+def dev_kernel(slots, dev_tok, slot_ref, local_ref, count_ref, ctx_ref, pos_ref, gain_ref, upd_ref, sq_ref, kv, dev, sems):
     entries = REQ_DEV * slots
     doc_len, width = ctx_ref.shape[1:]
     head_dim = width // 2
-    dev_tok = pos_ref.shape[0] // entries
     group = slots // GROUPS
     scale = head_dim ** (-0.5)
 
@@ -148,17 +203,24 @@
     for e in range(entries):
         bring(e).start()
     upd_ref[...] = jnp.zeros_like(upd_ref)
-    token = lax.broadcasted_iota(jnp.int32, (dev_tok, doc_len), 1)
+    sq_ref[...] = jnp.zeros_like(sq_ref)
+    token = lax.broadcasted_iota(jnp.int32, (doc_len, 128), 0)
+    lane_slot = lax.broadcasted_iota(jnp.int32, (1, group * dev_tok), 1) // dev_tok
     for r in range(REQ_DEV):
         count = count_ref[r]
         base = r * slots * doc_len
         for e in range(r * slots, (r + 1) * slots):
             bring(e).wait()
         for e in range(r * slots, (r + 1) * slots):
-            hot = (pos_ref[e * dev_tok : (e + 1) * dev_tok] == token).astype(jnp.bfloat16)
-            dev[e * dev_tok : (e + 1) * dev_tok] = jnp.dot(
-                hot, kv[e * doc_len : (e + 1) * doc_len], preferred_element_type=jnp.float32
+            where = pos_ref[pl.ds(slot_ref[e] * 8 + local_ref[e], 1)]
+            hot = (where == token).astype(jnp.bfloat16)
+            rows_of = lax.dot_general(
+                hot,
+                kv[e * doc_len : (e + 1) * doc_len],
+                (((0,), (0,)), ((), ())),
+                preferred_element_type=jnp.float32,
             )
+            dev[e * dev_tok : (e + 1) * dev_tok] = rows_of[:dev_tok]
         for g in range(GROUPS):
             first = r * slots + g * group
             rows = slice(first * dev_tok, (first + group) * dev_tok)
@@ -188,7 +250,10 @@
                 delta = gain_ref[...] * (summed / total)
                 fresh = mine + delta
                 square = jnp.sum(delta * delta, axis=1, keepdims=True) * (1.0 / width)
-                sq_ref[rows] = jnp.broadcast_to(square, (group * dev_tok, 128))
+                across_lanes = jnp.broadcast_to(square, (group * dev_tok, 128)).T[:1]
+                sq_ref[r * GROUPS + g : r * GROUPS + g + 1, : group * dev_tok] = jnp.where(
+                    lane_slot + g * group < count, across_lanes, 0.0
+                )
                 for i in range(group):
 
                     @pl.when(g * group + i < count)
@@ -198,22 +263,17 @@
                             [one[:, :head_dim], one[:, head_dim:]], axis=0
                         ).astype(jnp.bfloat16)
 
-            @pl.when(g * group >= count)
-            def _():
-                sq_ref[rows] = jnp.zeros((group * dev_tok, 128), jnp.float32)
-
-
-def deviations(slots, slot_of, counts, ctx, pos, gain):
+
+def deviations(slots, dev_tok, slot_of, local, counts, ctx, pos, gain):
     entries = REQ_DEV * slots
     peers, doc_len, width = ctx.shape
-    dev_tok = pos.shape[0] // entries
     return pl.pallas_call(
-        functools.partial(dev_kernel, slots),
+        functools.partial(dev_kernel, slots, dev_tok),
         out_shape=(
             jax.ShapeDtypeStruct((peers, 2 * dev_tok, width // 2), jnp.bfloat16),
-            jax.ShapeDtypeStruct((entries * dev_tok, 128), jnp.float32),
-        ),
-        in_specs=[whole(SMEM), whole(SMEM), whole(pl.ANY), whole(VMEM), whole(VMEM)],
+            jax.ShapeDtypeStruct((REQ_DEV * GROUPS, 128), jnp.float32),
+        ),
+        in_specs=[whole(SMEM), whole(SMEM), whole(SMEM), whole(pl.ANY), whole(VMEM), whole(VMEM)],
         out_specs=(whole(VMEM), whole(VMEM)),
         scratch_shapes=[
             VMEM((entries * doc_len, width), jnp.bfloat16),
@@ -225,11 +285,31 @@
             flops=2 * 2 * 480 * 2560 * 384, bytes_accessed=5 * 10**6, transcendentals=2 * 10**6
         ),
         name="deviations",
-    )(slot_of, counts, ctx, pos, gain)
+    )(slot_of, local, counts, ctx, pos, gain)
 
 
 def attend_kernel(
-    ny, slots, slot_ref, count_ref, ctx_ref, upd_ref, q_ref, own_ref, att_ref, ret_ref, ctx, kv, send, recv, local_sem
+    ny,
+    nh,
+    slots,
+    slot_ref,
+    count_ref,
+    ctx_ref,
+    upd_ref,
+    sq_ref,
+    q_ref,
+    own_ref,
+    att_ref,
+    ret_ref,
+    sum_ref,
+    ctx,
+    kv,
+    parts,
+    send,
+    recv,
+    hsend,
+    hrecv,
+    local_sem,
 ):
     peers, doc_len, width = ctx_ref.shape
     head_dim = width // 2
@@ -254,7 +334,11 @@
         return carry
 
     lax.fori_loop(1, peers, greet, 0)
-    pl.semaphore_wait(barrier, peers - 1)
+    head_at = lax.axis_index("heads")
+    fellows = [lax.rem(head_at + k, nh) for k in range(nh)]
+    for k in range(1, nh):
+        pl.semaphore_signal(barrier, inc=1, device_id={"heads": fellows[k]}, device_id_type=pl.DeviceIdType.MESH)
+    pl.semaphore_wait(barrier, peers + nh - 2)
 
     def back(s):
         return pltpu.make_async_remote_copy(
@@ -273,6 +357,20 @@
     lax.fori_loop(1, peers, launch, 0)
     mine = pltpu.make_async_copy(upd_ref.at[0], ret_ref.at[me], local_sem.at[1])
     mine.start()
+
+    def share(k):
+        return pltpu.make_async_remote_copy(
+            src_ref=sq_ref,
+            dst_ref=parts.at[head_at],
+            send_sem=hsend.at[k],
+            recv_sem=hrecv.at[k],
+            device_id={"heads": fellows[k]},
+            device_id_type=pl.DeviceIdType.MESH,
+        )
+
+    for k in range(1, nh):
+        share(k).start()
+    parts[head_at] = sq_ref[...]
 
     row = lax.broadcasted_iota(jnp.int32, (tokens, span - slots * doc_len), 0)
     col = lax.broadcasted_iota(jnp.int32, (tokens, span - slots * doc_len), 1)
@@ -325,28 +423,39 @@
         back(i).wait()
         return carry
 
+    for k in range(1, nh):
+        share(k).wait()
+    total = parts[0]
+    for k in range(1, nh):
+        total = total + parts[k]
+    sum_ref[...] = total * (1.0 / KVH)
     lax.fori_loop(1, peers, land, 0)
     mine.wait()
 
 
-def attend_and_return(slots, slot_of, counts, ctx, upd, queries, own):
+def attend_and_return(slots, slot_of, counts, ctx, upd, squares, queries, own):
     peers, doc_len, width = ctx.shape
     ny = peers // NZ
+    nh = lax.axis_size("heads")
     tokens = own.shape[0] // REQ_DEV
     span = slots * doc_len + (tokens + 127) // 128 * 128
     return pl.pallas_call(
-        functools.partial(attend_kernel, ny, slots),
+        functools.partial(attend_kernel, ny, nh, slots),
         out_shape=(
             jax.ShapeDtypeStruct(queries.shape, jnp.bfloat16),
             jax.ShapeDtypeStruct(upd.shape, jnp.bfloat16),
-        ),
-        in_specs=[whole(SMEM), whole(SMEM), whole(pl.ANY), whole(pl.ANY), whole(VMEM), whole(VMEM)],
-        out_specs=(whole(VMEM), whole(pl.ANY)),
+            jax.ShapeDtypeStruct(squares.shape, jnp.float32),
+        ),
+        in_specs=[whole(SMEM), whole(SMEM), whole(pl.ANY), whole(pl.ANY), whole(VMEM), whole(VMEM), whole(VMEM)],
+        out_specs=(whole(VMEM), whole(pl.ANY), whole(VMEM)),
         scratch_shapes=[
             VMEM(ctx.shape, ctx.dtype),
             VMEM((span, width), ctx.dtype),
+            VMEM((nh,) + squares.shape, squares.dtype),
             pltpu.SemaphoreType.DMA((peers,)),
             pltpu.SemaphoreType.DMA((peers,)),
+            pltpu.SemaphoreType.DMA((nh,)),
+            pltpu.SemaphoreType.DMA((nh,)),
             pltpu.SemaphoreType.DMA((2,)),
         ],
         compiler_params=pltpu.CompilerParams(
@@ -356,7 +465,7 @@
             flops=9 * 10**9, bytes_accessed=100 * 10**6, transcendentals=9 * 10**6
         ),
         name="attend_and_return",
-    )(slot_of, counts, ctx, upd, queries, own)
+    )(slot_of, counts, ctx, upd, squares, queries, own)
 
 
 def shards(queries, own_kv, cache, doc_lists, doc_counts, dev_pos, blend_gain):
@@ -384,14 +493,14 @@
     slot_of = ((y - owner // NZ) % ny) * NZ + (z - owner % NZ) % NZ
     counts = lax.dynamic_slice_in_dim(doc_counts, me * REQ_DEV, REQ_DEV, 0)
 
-    all_pos = lax.all_gather(dev_pos, "docs", axis=0, tiled=True)
-    ctx = gather_docs(sel.astype(jnp.int32), cache.reshape(DOC_DEV, doc_len, width))
-    pos = jnp.broadcast_to(all_pos[mine].reshape(-1, 1), (entries * dev_tok, doc_len))
-    upd, squares = deviations(slots, slot_of, counts, ctx, pos, blend_gain)
-    scores = lax.psum(squares[:, 0], "heads") / KVH
-    live = jnp.arange(slots, dtype=jnp.int32)[None, :] < counts[:, None]
-    dev_score = jnp.where(live[:, :, None], scores.reshape(REQ_DEV, slots, dev_tok), 0.0)
-    att, ret = attend_and_return(slots, slot_of, counts, ctx, upd, queries, own_kv)
+    pos = jnp.pad(dev_pos, ((0, 8 - DOC_DEV), (0, 128 - dev_tok)), constant_values=-1)
+    ctx, all_pos = gather_docs(sel.astype(jnp.int32), cache.reshape(DOC_DEV, doc_len, width), pos)
+    upd, squares = deviations(
+        slots, dev_tok, slot_of, mine % DOC_DEV, counts, ctx, all_pos.reshape(peers * 8, 128), blend_gain
+    )
+    att, ret, sums = attend_and_return(slots, slot_of, counts, ctx, upd, squares, queries, own_kv)
+    group_rows = slots // GROUPS * dev_tok
+    dev_score = sums.reshape(REQ_DEV, GROUPS, 128)[:, :, :group_rows].reshape(REQ_DEV, slots, dev_tok)
     returned = jnp.concatenate([ret[:, :dev_tok], ret[:, dev_tok:]], axis=2)
     return att, returned, dev_score
 

time: 237 us -> 158 us (0.67)
  blocking collectives: 91.2 us -> 0 us
  Pallas kernels: 131 us -> 148 us
  local copies, waits for them, and re-layouts: 9 us -> 5.83 us
    all_gather x1 -> x0, blocking collectives: 81.2 us -> none  [shards(): all_pos = lax.all_gather(dev_pos, 'docs', axis=0, tiled=True)]
    pallas_call x3, Pallas kernels: 131 us -> 148 us  [the longest x1 89.9 us: gather_docs(): pl.pallas_call(functools.partial(gather_kernel, ny), out_shape=(jax.Shape...]
    psum x1 -> x0, blocking collectives: 10 us -> none  [shards(): scores = lax.psum(squares[:, 0], 'heads') / KVH]
    unnamed x20 -> x11, local copies, waits for them, and re-layouts: 7.47 us -> 4 us
where the time goes in v2:
time: 158 us; the launch traced here: 156 us
  Pallas kernels  148 us (94%)
  local copies, waits for them, and re-layouts  5.83 us (4%)
    pallas_call x1, Pallas kernels, gather_docs(): pl.pallas_call(functools.partial(gather_kernel, ny), out_shape=(jax.Shape...  89.9 us
    pallas_call x1, Pallas kernels, attend_and_return(): pl.pallas_call(functools.partial(attend_kernel, ny, nh, slots), out_shape...  49.6 us
    pallas_call x1, Pallas kernels, deviations(): pl.pallas_call(functools.partial(dev_kernel, slots, dev_tok), out_shape=(...  8.78 us
    unnamed x11, local copies, waits for them, and re-layouts  4 us

profile of v2, /device:TPU:6, one launch (start us, length us, event | category | flops | bytes accessed | tf_op | source)
XLA Modules:
  0.0 156.1 jit_solution(13682010533962216576)
XLA Ops:
  0.7 0.7 dynamic_slice.14.count_ref
  1.4 0.7 pad.4.pos_ref
  2.1 0.8 copy.13
  2.9 0.1 reshape_reshape.3
  3.0 0.1 reshape.49
  3.2 0.2 select_reduce_fusion
  3.4 0.1 reshape.50.sel_ref
  3.5 0.0 copy-start
  3.5 1.0 copy-done
  4.5 89.9 %gather_docs.1 = (bf16[64,128,256]{2,1,0:T(8,128)(2,1)S(1)}, s32[4,16,8,128]{3,2,1,0:T(8,128)S(1)}) custom-call(s32[64]{0:T(128)S(1)} %reshape.50.sel_ref, bf16[6,128,256]{2,1,0:T(8,128)(2,1)S(1)} %bitcast.20, s32[8,128]{1,0:T(8,128)S(1)} %pad.4.pos_ref), custom_call_target="tpu_custom_call" | custom-call | bytes 200000000 | tf_op jit(solution)/shard_map/gather_docs/pallas_call | solution.py:163
  94.4 0.0 copy-start.3
  94.4 0.7 copy-done.3
  95.1 0.0 copy-start.1
  95.1 0.0 copy-start.2
  95.1 8.8 %deviations.1 = (bf16[64,48,128]{2,1,0:T(8,128)(2,1)S(1)}, f32[8,128]{1,0:T(8,128)S(1)}) custom-call(s32[40]{0:T(128)S(1)} %get-tuple-element.26.slot_ref, s32[40]{0:T(128)S(1)} %get-tuple-element.25.local_ref, s32[2]{0:T(128)S(1)} %dynamic_slice.14.count_ref, bf16[64,128,256]{2,1,0:T(8,128)(2,1)S(1)} %get-tuple-element.10.ctx_ref, s32[512,128]{1,0:T(8,128)S(1)} %bitcast.22, ...), custom_call_target="tpu_custom_call" | custom-call | flops 1887436800 | bytes 5000000 | tf_op jit(solution)/shard_map/deviations/pallas_call | solution.py:270
  103.9 0.0 copy-done.1
  103.9 0.0 copy-done.2
  103.9 49.6 %attend_and_return.1 = (bf16[384,1024]{1,0:T(8,128)(2,1)S(1)}, bf16[64,48,128]{2,1,0:T(8,128)(2,1)S(1)}, f32[8,128]{1,0:T(8,128)S(1)}) custom-call(s32[40]{0:T(128)S(1)} %get-tuple-element.26.slot_ref, s32[2]{0:T(128)S(1)} %dynamic_slice.14.count_ref, bf16[64,128,256]{2,1,0:T(8,128)(2,1)S(1)} %get-tuple-element.10.ctx_ref, ...), custom_call_target="tpu_custom_call" | custom-call | flops 8999999488 | bytes 100000000 | tf_op jit(solution)/shard_map/attend_and_return/pallas_call | solution.py:442
  153.5 0.1 reshape.54
  153.6 0.6 copy.15
  154.2 0.1 fusion.9
  154.3 1.0 pad_maximum_fusion
  155.2 0.9 copy.17
  (5 shorter events, 0.1 us)
Async XLA Ops:
  3.5 1.0 copy-start
  94.4 0.7 copy-start.3
  95.1 8.8 %copy-start.1 = (bf16[384,1024]{1,0:T(8,128)(2,1)S(1)}, bf16[384,1024]{1,0:T(8,128)(2,1)}, u32[]{:S(2)}) copy-start(bf16[384,1024]{1,0:T(8,128)(2,1)} %q_ref.1) | copy-start | bytes 2359300
  95.1 8.8 %copy-start.2 = (bf16[384,256]{1,0:T(8,128)(2,1)S(1)}, bf16[384,256]{1,0:T(8,128)(2,1)}, u32[]{:S(2)}) copy-start(bf16[384,256]{1,0:T(8,128)(2,1)} %own_ref.1) | copy-start | bytes 589828

commit v3 on v2

v3 whole, which is shorter than its diff:
```python
import functools

import jax
import jax.numpy as jnp
from jax import lax
from jax.experimental import pallas as pl
from jax.experimental.pallas import tpu as pltpu
from jax.sharding import PartitionSpec as P

KVH = 8
REQ_DEV = 2
DOC_DEV = 6
NZ = 16
very_low = -1e30
VMEM = pltpu.VMEM
SMEM = pltpu.SMEM
LOG2E = 1.4426950408889634
GROUPS = 4
WINDOW = 3


def whole(space):
    return pl.BlockSpec(memory_space=space)


def place(ny, y, z):
    return lax.rem(y + 2 * ny, ny) * NZ + lax.rem(z + 2 * NZ, NZ)


def gather_kernel(ny, sel_ref, cache_ref, pos_ref, ctx_ref, allpos_ref, *scratch):
    half = NZ // 2
    full = half - 1
    plus = scratch[:full]
    minus = scratch[full : 2 * full]
    far, picked, relay, ring_pos, zsend, zrecv, ysend, yrecv, fsend, frecv, psend, precv, local_sem = scratch[2 * full :]
    me = lax.axis_index("docs")
    y, z = me // NZ, lax.rem(me, NZ)
    part = DOC_DEV // 2

    barrier = pltpu.get_barrier_semaphore()
    partners = [place(ny, y, z + 1), place(ny, y, z - 1)]
    partners += [place(ny, y + t, z) for t in range(1, ny)]
    for partner in partners:
        pl.semaphore_signal(barrier, inc=1, device_id={"docs": partner}, device_id_type=pl.DeviceIdType.MESH)
    ring_pos[0] = pos_ref[...]
    pl.semaphore_wait(barrier, len(partners))

    order = [(step, doc) for step in range(1, half) for doc in range(DOC_DEV)]
    orders = [order + [(half, way * part + doc) for doc in range(part)] for way in range(2)]

    def ring(way, step, doc):
        bufs = plus if way == 0 else minus
        src = cache_ref if step == 1 else bufs[step - 2]
        dst = far if step == half else bufs[step - 1]
        return pltpu.make_async_remote_copy(
            src_ref=src.at[doc],
            dst_ref=dst.at[doc],
            send_sem=zsend.at[way, step - 1, doc],
            recv_sem=zrecv.at[way, step - 1, doc],
            device_id={"docs": partners[way]},
            device_id_type=pl.DeviceIdType.MESH,
        )

    def ring_of_pos(way, step):
        src, dst = (step - 1, step) if way == 0 else ((NZ - step + 1) % NZ, NZ - step)
        return pltpu.make_async_remote_copy(
            src_ref=ring_pos.at[src],
            dst_ref=ring_pos.at[dst],
            send_sem=psend.at[way, step],
            recv_sem=precv.at[way, step],
            device_id={"docs": partners[way]},
            device_id_type=pl.DeviceIdType.MESH,
        )

    def pos_across(t):
        return pltpu.make_async_remote_copy(
            src_ref=ring_pos,
            dst_ref=allpos_ref.at[t],
            send_sem=psend.at[0, half + t],
            recv_sem=precv.at[0, half + t],
            device_id={"docs": place(ny, y + t, z)},
            device_id_type=pl.DeviceIdType.MESH,
        )

    def aside(j):
        return partners[2] if j % 2 == 0 else partners[ny]

    def across(t, j):
        middle = 2 * t == ny
        return pltpu.make_async_remote_copy(
            src_ref=picked.at[t, j],
            dst_ref=relay.at[j] if middle else ctx_ref.at[t * NZ + j],
            send_sem=ysend.at[t, j],
            recv_sem=frecv.at[j] if middle else yrecv.at[t, j],
            device_id={"docs": aside(j) if middle else place(ny, y + t, z)},
            device_id_type=pl.DeviceIdType.MESH,
        )

    def forward(j):
        return pltpu.make_async_remote_copy(
            src_ref=relay.at[j],
            dst_ref=ctx_ref.at[ny // 2 * NZ + j],
            send_sem=fsend.at[j],
            recv_sem=yrecv.at[ny // 2, j],
            device_id={"docs": aside(j)},
            device_id_type=pl.DeviceIdType.MESH,
        )

    def keep(j):
        return pltpu.make_async_copy(picked.at[0, j], ctx_ref.at[j], local_sem.at[j])

    keep_pos = pltpu.make_async_copy(ring_pos, allpos_ref.at[0], local_sem.at[NZ])

    waiting = []

    def pass_on():
        for j in waiting:
            across(ny // 2, j).wait_recv()
            forward(j).start()
        waiting.clear()

    def pick(buf, j):
        for t in [ny // 2] + [t for t in range(1, ny) if 2 * t != ny] + [0]:
            picked[t, j] = buf[sel_ref[t * NZ + j]]
            if t:
                across(t, j).start()
            else:
                keep(j).start()

    for n in range(len(orders[0])):
        for way in range(2):
            step, doc = orders[way][n]
            if step > 1:
                ring(way, step - 1, doc).wait_recv()
            if n >= WINDOW:
                ring(way, *orders[way][n - WINDOW]).wait_send()
            ring(way, step, doc).start()
        step, doc = order[n] if n < len(order) else (half, n - len(order))
        if doc == 0:
            for way in range(2):
                if step > 1 and (way == 0 or step <= half):
                    ring_of_pos(way, step - 1).wait_recv()
                if way == 0 or step < half:
                    ring_of_pos(way, step).start()
        if n == WINDOW - 1:
            pick(cache_ref, 0)
            waiting.append(0)
        if step > 1 and step < half and doc == DOC_DEV - 1:
            pass_on()
            waiting.extend([step - 1, NZ - step + 1])
            pick(plus[step - 2], step - 1)
            pick(minus[step - 2], NZ - step + 1)
    for way in range(2):
        for doc in range(DOC_DEV):
            if not part * way <= doc < part * (way + 1):
                ring(way, full, doc).wait_recv()
    pass_on()
    pick(plus[full - 1], full)
    pick(minus[full - 1], NZ - full)
    waiting.extend([full, NZ - full])
    ring_of_pos(0, half).wait_recv()
    for t in range(1, ny):
        pos_across(t).start()
    keep_pos.start()
    for way in range(2):
        for doc in range(part):
            ring(way, half, way * part + doc).wait_recv()
    pick(far, half)
    waiting.append(half)
    pass_on()
    for way in range(2):
        for n in range(len(orders[way]) - WINDOW, len(orders[way])):
            ring(way, *orders[way][n]).wait_send()
        for step in range(1, half + 1):
            if way == 0 or step < half:
                ring_of_pos(way, step).wait_send()
    for j in range(NZ):
        for t in range(1, ny):
            across(t, j).wait_send()
            if 2 * t == ny:
                forward(j).wait()
            else:
                across(t, j).wait_recv()
        keep(j).wait()
    for t in range(1, ny):
        pos_across(t).wait()
    keep_pos.wait()


def gather_docs(sel, cache, pos):
    peers = lax.axis_size("docs")
    ny = peers // NZ
    full = NZ // 2 - 1
    block = cache.shape
    one = block[1:]
    return pl.pallas_call(
        functools.partial(gather_kernel, ny),
        out_shape=(
            jax.ShapeDtypeStruct((peers,) + one, cache.dtype),
            jax.ShapeDtypeStruct((ny, NZ) + pos.shape, pos.dtype),
        ),
        in_specs=[whole(SMEM), whole(VMEM), whole(VMEM)],
        out_specs=(whole(pl.ANY), whole(pl.ANY)),
        scratch_shapes=[VMEM(block, cache.dtype)] * (2 * full + 1)
        + [
            VMEM((ny, NZ) + one, cache.dtype),
            VMEM((NZ,) + one, cache.dtype),
            VMEM((NZ,) + pos.shape, pos.dtype),
            pltpu.SemaphoreType.DMA((2, NZ // 2, DOC_DEV)),
            pltpu.SemaphoreType.DMA((2, NZ // 2, DOC_DEV)),
            pltpu.SemaphoreType.DMA((ny, NZ)),
            pltpu.SemaphoreType.DMA((ny, NZ)),
            pltpu.SemaphoreType.DMA((NZ,)),
            pltpu.SemaphoreType.DMA((NZ,)),
            pltpu.SemaphoreType.DMA((2, NZ // 2 + ny)),
            pltpu.SemaphoreType.DMA((2, NZ // 2 + ny)),
            pltpu.SemaphoreType.DMA((NZ + 1,)),
        ],
        compiler_params=pltpu.CompilerParams(
            collective_id=0, has_side_effects=True, vmem_limit_bytes=24 * 2**20
        ),
        cost_estimate=pl.CostEstimate(flops=0, bytes_accessed=200 * 10**6, transcendentals=0),
        name="gather_docs",
    )(sel, cache, pos)


def finish_kernel(
    ny,
    nh,
    slots,
    dev_tok,
    slot_ref,
    local_ref,
    inv_ref,
    count_ref,
    ctx_ref,
    pos_ref,
    gain_ref,
    q_ref,
    own_ref,
    att_ref,
    ret_ref,
    sum_ref,
    kv,
    dev,
    fresh,
    upd,
    squares,
    parts,
    relay,
    send,
    recv,
    fsend,
    frecv,
    hsend,
    hrecv,
    local_sem,
):
    entries = REQ_DEV * slots
    peers, doc_len, width = ctx_ref.shape
    head_dim = width // 2
    tokens = own_ref.shape[0] // REQ_DEV
    heads = q_ref.shape[1] // head_dim
    context = slots * doc_len
    span = kv.shape[1]
    group = slots // GROUPS
    scale = head_dim ** (-0.5)
    half = NZ // 2
    me = lax.axis_index("docs")
    y, z = me // NZ, lax.rem(me, NZ)
    head_at = lax.axis_index("heads")
    fellows = [lax.rem(head_at + k, nh) for k in range(nh)]
    barrier = pltpu.get_barrier_semaphore()

    def holder(s):
        return place(ny, y - s // NZ, z - lax.rem(s, NZ))

    def greet(s, carry):
        pl.semaphore_signal(barrier, inc=1, device_id={"docs": holder(s)}, device_id_type=pl.DeviceIdType.MESH)
        return carry

    lax.fori_loop(1, peers, greet, 0)
    for k in range(1, nh):
        pl.semaphore_signal(barrier, inc=1, device_id={"heads": fellows[k]}, device_id_type=pl.DeviceIdType.MESH)

    token = lax.broadcasted_iota(jnp.int32, (doc_len, 128), 0)
    lane_slot = lax.broadcasted_iota(jnp.int32, (1, group * dev_tok), 1) // dev_tok
    squares[...] = jnp.zeros_like(squares)
    fresh[entries] = jnp.zeros(fresh.shape[1:], fresh.dtype)
    for r in range(REQ_DEV):
        kv[r, context:] = jnp.zeros((span - context, width), kv.dtype)
        kv[r, context : context + tokens] = own_ref[r * tokens : (r + 1) * tokens]
        for k in range(slots):
            e = r * slots + k
            doc = ctx_ref[slot_ref[e]]
            kv[r, k * doc_len : (k + 1) * doc_len] = doc
            where = pos_ref[pl.ds(slot_ref[e] * 8 + local_ref[e], 1)]
            hot = (where == token).astype(jnp.bfloat16)
            rows_of = lax.dot_general(hot, doc, (((0,), (0,)), ((), ())), preferred_element_type=jnp.float32)
            dev[e * dev_tok : (e + 1) * dev_tok] = rows_of[:dev_tok]
    for r in range(REQ_DEV):
        for g in range(GROUPS):
            first = r * slots + g * group
            known = (g + 1) * group * doc_len
            mine = dev[first * dev_tok : (first + group) * dev_tok]
            scores = lax.dot_general(
                mine[:, :head_dim].astype(jnp.bfloat16),
                kv[r, :known, :head_dim],
                (((1,), (1,)), ((), ())),
                preferred_element_type=jnp.float32,
            )
            shape = (group * dev_tok, group * doc_len)
            row_slot = lax.broadcasted_iota(jnp.int32, shape, 0) // dev_tok
            key_slot = lax.broadcasted_iota(jnp.int32, shape, 1) // doc_len
            last = jnp.where(row_slot >= key_slot, scores[:, known - shape[1] :], very_low)
            scores = last if g == 0 else jnp.concatenate([scores[:, : known - shape[1]], last], axis=1)
            top = jnp.max(scores, axis=1, keepdims=True)
            weights = jnp.exp2((scores - top) * (scale * LOG2E))
            total = jnp.sum(weights, axis=1, keepdims=True)
            summed = jnp.dot(weights.astype(jnp.bfloat16), kv[r, :known], preferred_element_type=jnp.float32)
            delta = gain_ref[...] * (summed / total)
            renewed = mine + delta
            square = jnp.sum(delta * delta, axis=1, keepdims=True) * (1.0 / width)
            across_lanes = jnp.broadcast_to(square, (group * dev_tok, 128)).T[:1]
            squares[r * GROUPS + g : r * GROUPS + g + 1, : group * dev_tok] = jnp.where(
                lane_slot + g * group < count_ref[me * REQ_DEV + r], across_lanes, 0.0
            )
            for i in range(group):
                one = renewed[i * dev_tok : (i + 1) * dev_tok]
                fresh[first + i] = jnp.concatenate([one[:, :head_dim], one[:, head_dim:]], axis=0).astype(
                    jnp.bfloat16
                )

    pl.semaphore_wait(barrier, peers + nh - 2)

    def back(s):
        return pltpu.make_async_remote_copy(
            src_ref=upd.at[s],
            dst_ref=ret_ref.at[me],
            send_sem=send.at[s],
            recv_sem=recv.at[s],
            device_id={"docs": holder(s)},
            device_id_type=pl.DeviceIdType.MESH,
        )

    def aside(t):
        s = t * NZ + half
        turn = 1 - 2 * (t % 2)
        return pltpu.make_async_remote_copy(
            src_ref=upd.at[s],
            dst_ref=relay.at[t],
            send_sem=send.at[s],
            recv_sem=frecv.at[t],
            device_id={"docs": place(ny, y, z + turn)},
            device_id_type=pl.DeviceIdType.MESH,
        )

    def forward(t):
        turn = 1 - 2 * (t % 2)
        return pltpu.make_async_remote_copy(
            src_ref=relay.at[t],
            dst_ref=ret_ref.at[place(ny, y, z - turn)],
            send_sem=fsend.at[t],
            recv_sem=recv.at[t * NZ + half],
            device_id={"docs": place(ny, y - t, z - turn - half)},
            device_id_type=pl.DeviceIdType.MESH,
        )

    for t in range(ny):
        upd[t * NZ + half] = fresh[inv_ref[t * NZ + half]]
        aside(t).start()

    def far_first(i):
        k = i // ny
        j = jnp.where(k % 2 == 0, half - 1 - k // 2, half + 1 + k // 2)
        return lax.rem(i, ny) * NZ + j

    def launch(i, carry):
        s = far_first(i)
        upd[s] = fresh[inv_ref[s]]
        back(s).start()
        return carry

    lax.fori_loop(0, ny * (NZ - 2), launch, 0)
    for t in range(1, ny):
        upd[t * NZ] = fresh[inv_ref[t * NZ]]
        back(t * NZ).start()
    ret_ref[me] = fresh[inv_ref[0]]

    def share(k):
        return pltpu.make_async_remote_copy(
            src_ref=squares,
            dst_ref=parts.at[head_at],
            send_sem=hsend.at[k],
            recv_sem=hrecv.at[k],
            device_id={"heads": fellows[k]},
            device_id_type=pl.DeviceIdType.MESH,
        )

    for k in range(1, nh):
        share(k).start()
    parts[head_at] = squares[...]

    row = lax.broadcasted_iota(jnp.int32, (tokens, span - context), 0)
    col = lax.broadcasted_iota(jnp.int32, (tokens, span - context), 1)
    causal = row >= col
    place_of = lax.broadcasted_iota(jnp.int32, (1, context), 1)
    for r in range(REQ_DEV):
        live = place_of < count_ref[me * REQ_DEV + r] * doc_len

        def head(i, carry):
            cols = pl.ds(pl.multiple_of(i * head_dim, head_dim), head_dim)
            scores = lax.dot_general(
                q_ref[r * tokens : (r + 1) * tokens, cols],
                kv[r, :, :head_dim],
                (((1,), (1,)), ((), ())),
                preferred_element_type=jnp.float32,
            )
            docs = jnp.where(live, scores[:, :context], very_low)
            own = jnp.where(causal, scores[:, context:], very_low)
            top = jnp.maximum(jnp.max(docs, axis=1, keepdims=True), jnp.max(own, axis=1, keepdims=True))
            docs = jnp.exp2((docs - top) * (scale * LOG2E))
            own = jnp.exp2((own - top) * (scale * LOG2E))
            total = jnp.sum(docs, axis=1, keepdims=True) + jnp.sum(own, axis=1, keepdims=True)
            summed = jnp.dot(
                docs.astype(jnp.bfloat16), kv[r, :context, head_dim:], preferred_element_type=jnp.float32
            ) + jnp.dot(own.astype(jnp.bfloat16), kv[r, context:, head_dim:], preferred_element_type=jnp.float32)
            att_ref[r * tokens : (r + 1) * tokens, cols] = (summed / total).astype(jnp.bfloat16)
            return carry

        if r == 0:
            lax.fori_loop(0, 1, head, 0)
            for t in range(ny):
                aside(t).wait_recv()
                forward(t).start()
            lax.fori_loop(1, heads, head, 0)
        else:
            lax.fori_loop(0, heads, head, 0)

    for k in range(1, nh):
        share(k).wait()
    total = parts[0]
    for k in range(1, nh):
        total = total + parts[k]
    sum_ref[...] = total * (1.0 / KVH)

    def land(i, carry):
        back(far_first(i)).wait()
        return carry

    lax.fori_loop(0, ny * (NZ - 2), land, 0)
    for t in range(ny):
        if t:
            back(t * NZ).wait()
        aside(t).wait_send()
        forward(t).wait()


def finish(slots, dev_tok, slot_of, local, inv, counts, ctx, pos, gain, queries, own):
    peers, doc_len, width = ctx.shape
    ny = peers // NZ
    nh = lax.axis_size("heads")
    entries = REQ_DEV * slots
    tokens = own.shape[0] // REQ_DEV
    span = slots * doc_len + (tokens + 127) // 128 * 128
    packet = (2 * dev_tok, width // 2)
    square = jax.ShapeDtypeStruct((REQ_DEV * GROUPS, 128), jnp.float32)
    return pl.pallas_call(
        functools.partial(finish_kernel, ny, nh, slots, dev_tok),
        out_shape=(
            jax.ShapeDtypeStruct(queries.shape, jnp.bfloat16),
            jax.ShapeDtypeStruct((peers,) + packet, jnp.bfloat16),
            square,
        ),
        in_specs=[whole(SMEM)] * 4 + [whole(VMEM)] * 5,
        out_specs=(whole(VMEM), whole(VMEM), whole(VMEM)),
        scratch_shapes=[
            VMEM((REQ_DEV, span, width), ctx.dtype),
            VMEM((entries * dev_tok, width), jnp.float32),
            VMEM((entries + 1,) + packet, jnp.bfloat16),
            VMEM((peers,) + packet, jnp.bfloat16),
            VMEM(square.shape, square.dtype),
            VMEM((nh,) + square.shape, square.dtype),
            VMEM((ny,) + packet, jnp.bfloat16),
            pltpu.SemaphoreType.DMA((peers,)),
            pltpu.SemaphoreType.DMA((peers,)),
            pltpu.SemaphoreType.DMA((ny,)),
            pltpu.SemaphoreType.DMA((ny,)),
            pltpu.SemaphoreType.DMA((nh,)),
            pltpu.SemaphoreType.DMA((nh,)),
            pltpu.SemaphoreType.DMA((2,)),
        ],
        compiler_params=pltpu.CompilerParams(
            collective_id=1, has_side_effects=True, vmem_limit_bytes=44 * 2**20
        ),
        cost_estimate=pl.CostEstimate(
            flops=9 * 10**9, bytes_accessed=100 * 10**6, transcendentals=9 * 10**6
        ),
        name="finish",
    )(slot_of, local, inv, counts, ctx, pos, gain, queries, own)


def shards(queries, own_kv, cache, doc_lists, doc_counts, dev_pos, blend_gain):
    width = blend_gain.shape[1]
    head_dim = width // 2
    peers = lax.axis_size("docs")
    ny = peers // NZ
    me = lax.axis_index("docs")
    y, z = me // NZ, me % NZ
    slots = doc_lists.shape[1]
    entries = REQ_DEV * slots
    dev_tok = dev_pos.shape[1]
    doc_len = cache.shape[0] // DOC_DEV
    combined = doc_lists.reshape(peers, entries)

    row_lists = jnp.roll(combined.reshape(ny, NZ, entries)[:, z], -y, axis=0)
    row_owner = row_lists // DOC_DEV
    steps = jnp.arange(NZ, dtype=jnp.int32)
    passing = y * NZ + (z - steps) % NZ
    hits = row_owner[:, :, None] == passing[None, None, :]
    sel = jnp.sum(jnp.where(hits, (row_lists % DOC_DEV)[:, :, None], 0), axis=1).reshape(-1)

    mine = combined[me]
    owner = mine // DOC_DEV
    slot_of = ((y - owner // NZ) % ny) * NZ + (z - owner % NZ) % NZ
    entry = jnp.arange(entries, dtype=jnp.int32)
    live = (jnp.arange(slots, dtype=jnp.int32)[None, :] < doc_counts.reshape(peers, REQ_DEV)[me][:, None]).reshape(-1)
    filled = (slot_of[None, :] == jnp.arange(peers, dtype=jnp.int32)[:, None]) & live[None, :]
    inv = entries + jnp.sum(jnp.where(filled, entry[None, :] - entries, 0), axis=1)

    pos = jnp.pad(dev_pos, ((0, 8 - DOC_DEV), (0, 128 - dev_tok)), constant_values=-1)
    ctx, all_pos = gather_docs(sel.astype(jnp.int32), cache.reshape(DOC_DEV, doc_len, width), pos)
    att, ret, sums = finish(
        slots,
        dev_tok,
        slot_of,
        mine % DOC_DEV,
        inv,
        doc_counts,
        ctx,
        all_pos.reshape(peers * 8, 128),
        blend_gain,
        queries,
        own_kv,
    )
    group_rows = slots // GROUPS * dev_tok
    dev_score = sums.reshape(REQ_DEV, GROUPS, 128)[:, :, :group_rows].reshape(REQ_DEV, slots, dev_tok)
    returned = jnp.concatenate([ret[:, :dev_tok], ret[:, dev_tok:]], axis=2)
    return att, returned, dev_score


def solution(mesh):
    return jax.shard_map(
        shards,
        mesh=mesh,
        in_specs=(
            P("docs", "heads"),
            P("docs", "heads"),
            P("docs", "heads"),
            P(),
            P(),
            P("docs", None),
            P("heads", None),
        ),
        out_specs=(P("docs", "heads"), P("docs", None, "heads"), P("docs", None, None)),
        check_vma=False,
    )
```

time: 158 us -> 152 us (0.962)
  Pallas kernels: 148 us -> 138 us
  local copies, waits for them, and re-layouts: 5.83 us -> 8.68 us
    pallas_call x2 -> x1, Pallas kernels: 58.3 us -> 45.1 us  [finish(): pl.pallas_call(functools.partial(finish_kernel, ny, nh, slots, dev_tok),...]
    pallas_call x1, Pallas kernels: 89.9 us -> 92.9 us  [gather_docs(): pl.pallas_call(functools.partial(gather_kernel, ny), out_shape=(jax.Shape...]
    unnamed x11 -> x13, local copies, waits for them, and re-layouts: 4 us -> 6.7 us
where the time goes in v3:
time: 152 us; the launch traced here: 149 us
  Pallas kernels  138 us (91%)
  local copies, waits for them, and re-layouts  8.68 us (6%)
    pallas_call x1, Pallas kernels, gather_docs(): pl.pallas_call(functools.partial(gather_kernel, ny), out_shape=(jax.Shape...  92.9 us
    pallas_call x1, Pallas kernels, finish(): pl.pallas_call(functools.partial(finish_kernel, ny, nh, slots, dev_tok),...  45.1 us
    unnamed x13, local copies, waits for them, and re-layouts  6.7 us

profile of v3, /device:TPU:6, one launch (start us, length us, event | category | flops | bytes accessed | tf_op | source)
XLA Modules:
  0.0 149.0 jit_solution(4795656324745347890)
XLA Ops:
  0.7 0.7 pad.4.pos_ref
  1.4 0.8 reshape.73
  2.2 0.1 iota_compare_fusion.1
  2.3 0.1 lt.93
  2.4 0.8 copy.13
  3.2 0.1 reshape.72
  3.3 0.1 reshape_reshape.3
  3.4 0.1 select_reduce_fusion.1
  3.6 0.2 select_reduce_fusion
  3.8 0.1 reshape.74.sel_ref
  3.9 0.0 copy-start
  3.9 1.0 copy-done
  4.9 92.9 %gather_docs.1 = (bf16[64,128,256]{2,1,0:T(8,128)(2,1)S(1)}, s32[4,16,8,128]{3,2,1,0:T(8,128)S(1)}) custom-call(s32[64]{0:T(128)S(1)} %reshape.74.sel_ref, bf16[6,128,256]{2,1,0:T(8,128)(2,1)S(1)} %bitcast.24, s32[8,128]{1,0:T(8,128)S(1)} %pad.4.pos_ref), custom_call_target="tpu_custom_call" | custom-call | bytes 200000000 | tf_op jit(solution)/shard_map/gather_docs/pallas_call | solution.py:196
  97.8 0.0 copy-start.1
  97.8 0.6 copy-done.1
  98.5 1.1 copy-done.2
  99.6 0.9 copy-done.3
  100.6 0.7 copy-done.4
  101.2 45.1 %finish.1 = (bf16[384,1024]{1,0:T(8,128)(2,1)S(1)}, bf16[64,48,128]{2,1,0:T(8,128)(2,1)S(1)}, f32[8,128]{1,0:T(8,128)S(1)}) custom-call(s32[40]{0:T(128)S(1)} %get-tuple-element.22.slot_ref, s32[40]{0:T(128)S(1)} %get-tuple-element.21.local_ref, s32[64]{0:T(128)S(1)} %broadcast_add_fusion.inv_ref, s32[128]{0:T(128)S(1)} %copy-done.1, ...), custom_call_target="tpu_custom_call" | custom-call | flops 8999999488 | bytes 100000000 | tf_op jit(solution)/shard_map/finish/pallas_call | solution.py:468
  146.4 0.1 reshape.78
  146.5 0.6 copy.15
  147.1 0.1 fusion.17
  147.2 1.0 pad_maximum_fusion
  148.1 0.9 copy.17
  (12 shorter events, 0.2 us)
Async XLA Ops:
  3.9 1.0 copy-start
  97.8 0.7 copy-start.1
  98.5 1.1 copy-start.2
  99.6 0.9 copy-start.3
  100.5 0.7 copy-start.4

commit v4 on v0

v4 whole, which is shorter than its diff:
```python
import functools

import jax
import jax.numpy as jnp
from jax import lax
from jax.experimental import pallas as pl
from jax.experimental.pallas import tpu as pltpu
from jax.sharding import PartitionSpec as P

KVH = 8
REQ_DEV = 2
DOC_DEV = 6
NZ = 16
very_low = -1e30
VMEM = pltpu.VMEM
SMEM = pltpu.SMEM
DMA = pltpu.SemaphoreType.DMA
MESH = pl.DeviceIdType.MESH
LOG2E = 1.4426950408889634
GROUPS = 4
CHUNKS = 3
KEY, VALUE = 0, 1


def whole(space):
    return pl.BlockSpec(memory_space=space)


def place(ny, y, z):
    return lax.rem(y + 2 * ny, ny) * NZ + lax.rem(z + 2 * NZ, NZ)


def blend_kernel(
    ny, nh, slots, dev_tok, names, table_ref, list_ref, count_ref, cache_ref, pos_ref, gain_ref, q_ref, own_ref,
    att_ref, retk_ref, retv_ref, sum_ref, *scratch
):
    has = dict(zip(names, scratch))
    peers = ny * NZ
    entries = REQ_DEV * slots
    doc_len, head_dim = has["base0"].shape[1:]
    tokens = own_ref.shape[0] // REQ_DEV
    heads = q_ref.shape[1] // head_dim
    context = slots * doc_len
    span = has["all0"].shape[1]
    group = slots // GROUPS
    scale = head_dim ** (-0.5)
    half = NZ // 2
    full = half - 1
    each = DOC_DEV // CHUNKS
    me = lax.axis_index("docs")
    y, z = me // NZ, lax.rem(me, NZ)
    head_at = lax.axis_index("heads")
    fellows = [lax.rem(head_at + k, nh) for k in range(nh)]
    ret = (retk_ref, retv_ref)
    local_sem = has["local_sem"]

    def two(name):
        return has[name + "0"], has[name + "1"]

    base, far, last_pick, picked, relay, ctx, every, fresh, upd, turn_buf = map(
        two, ("base", "far", "last", "picked", "relay", "ctx", "all", "fresh", "upd", "turn")
    )
    passing = [[[has["ring%d%d%d" % (p, way, s)] for s in range(full)] for way in range(2)] for p in range(2)]
    ring_pos, all_pos, dev, squares, parts = (has[n] for n in ("ring_pos", "all_pos", "dev", "squares", "parts"))
    weights_of = [has["weights%d" % g] for g in range(GROUPS)]
    totals, columns = has["totals"], has["columns"]

    fetch = [
        pltpu.make_async_copy(cache_ref.at[:, :, pl.ds(p * head_dim, head_dim)], base[p], local_sem.at[p])
        for p in range(2)
    ]
    fetch += [
        pltpu.make_async_copy(q_ref, has["q"], local_sem.at[2]),
        pltpu.make_async_copy(own_ref, has["own"], local_sem.at[3]),
    ]
    for one in fetch:
        one.start()
    barrier = pltpu.get_barrier_semaphore()

    def holder(s):
        return place(ny, y - s // NZ, z - lax.rem(s, NZ))

    def greet(s, carry):
        pl.semaphore_signal(barrier, inc=1, device_id={"docs": holder(s)}, device_id_type=MESH)
        return carry

    lax.fori_loop(1, peers, greet, 0)
    for k in range(1, nh):
        pl.semaphore_signal(barrier, inc=1, device_id={"heads": fellows[k]}, device_id_type=MESH)
    ring_pos[0] = jnp.full(ring_pos.shape[1:], -1, jnp.int32)
    ring_pos[0, :DOC_DEV, :dev_tok] = pos_ref[...]
    squares[...] = jnp.zeros_like(squares)
    for p in range(2):
        fresh[p][entries] = jnp.zeros(fresh[p].shape[1:], fresh[p].dtype)
        every[p][...] = jnp.zeros_like(every[p])
    fetch[KEY].wait()
    pl.semaphore_wait(barrier, peers + nh - 2)

    along_z = [place(ny, y, z + 1), place(ny, y, z - 1)]
    along_y = [place(ny, y + t, z) for t in range(ny)]

    def remote(src, dst, send_sem, recv_sem, device):
        return pltpu.make_async_remote_copy(
            src_ref=src, dst_ref=dst, send_sem=send_sem, recv_sem=recv_sem,
            device_id={"docs": device}, device_id_type=MESH,
        )

    def ring(p, way, step, chunk):
        src = base[p] if step == 1 else passing[p][way][step - 2]
        rows = pl.ds(chunk * each, each)
        sems = has["zsend"].at[p, way, step - 1, chunk], has["zrecv"].at[p, way, step - 1, chunk]
        return remote(src.at[rows], passing[p][way][step - 1].at[rows], *sems, along_z[way])

    def last_hop(p, t):
        sems = has["lsend"].at[p, t], has["lrecv"].at[p, t]
        return remote(last_pick[p].at[t], far[p].at[t], *sems, along_z[2 * t // ny])

    def ring_of_pos(way, step):
        src, dst = (step - 1, step) if way == 0 else ((NZ - step + 1) % NZ, NZ - step)
        sems = has["psend"].at[way, step], has["precv"].at[way, step]
        return remote(ring_pos.at[src], ring_pos.at[dst], *sems, along_z[way])

    def pos_across(t):
        sems = has["psend"].at[0, half + t], has["precv"].at[0, half + t]
        return remote(ring_pos, all_pos.at[t], *sems, along_y[t])

    def aside(j):
        return along_y[1] if j % 2 == 0 else along_y[ny - 1]

    def relayed(t, j):
        return 2 * t == ny and j != half

    def across(p, t, j):
        src = far[p].at[t] if j == half else picked[p].at[t, j]
        dst = relay[p].at[j] if relayed(t, j) else ctx[p].at[t * NZ + j]
        recv = has["frecv"].at[p, j] if relayed(t, j) else has["yrecv"].at[p, t, j]
        return remote(src, dst, has["ysend"].at[p, t, j], recv, aside(j) if relayed(t, j) else along_y[t])

    def forward(p, j):
        sems = has["fsend"].at[p, j], has["yrecv"].at[p, ny // 2, j]
        return remote(relay[p].at[j], ctx[p].at[ny // 2 * NZ + j], *sems, aside(j))

    waiting = []

    def pass_on():
        for p, j in waiting:
            across(p, ny // 2, j).wait_recv()
            forward(p, j).start()
        waiting.clear()

    def pick(p, buf, j):
        for t in [ny // 2] + [t for t in range(1, ny) if 2 * t != ny] + [0]:
            doc = buf[lax.rem(table_ref[t * NZ + j], 8)]
            if t:
                picked[p][t, j] = doc
                across(p, t, j).start()
            else:
                ctx[p][j] = doc
        waiting.append((p, j))

    def begin(p):
        for chunk in range(CHUNKS):
            for way in range(2):
                ring(p, way, 1, chunk).start()

    def travel(p, tasks):
        todo = list(tasks)
        for step in range(1, half):
            for chunk in range(CHUNKS):
                for way in range(2):
                    ring(p, way, step, chunk).wait_recv()
                    if step < full:
                        ring(p, way, step + 1, chunk).start()
                if p == KEY and chunk == 0:
                    for way in range(2):
                        ring_of_pos(way, step).wait_recv()
                        if way == 0 or step < full:
                            ring_of_pos(way, step + 1).start()
                if chunk < CHUNKS - 1 and todo:
                    todo.pop(0)()
            if step == full:
                for t in range(ny):
                    buf = passing[p][2 * t // ny][full - 1]
                    last_pick[p][t] = buf[lax.rem(table_ref[2 * peers + t], 8)]
                    last_hop(p, t).start()
                if p == KEY:
                    fetch[VALUE].wait()
                    begin(VALUE)
            pass_on()
            pick(p, passing[p][0][step - 1], step)
            pick(p, passing[p][1][step - 1], NZ - step)
            if todo:
                todo.pop(0)()
        for task in todo:
            task()

    def arrive(p):
        for t in range(ny):
            last_hop(p, t).wait_recv()
        pass_on()
        for t in range(1, ny):
            across(p, t, half).start()
        ctx[p][half] = far[p][0]
        if p == KEY:
            ring_of_pos(0, half).wait_recv()
            for t in range(1, ny):
                pos_across(t).start()
            all_pos[0] = ring_pos[...]

    def slot_of(e):
        named = list_ref[e % slots, me * REQ_DEV + e // slots]
        owner = named // DOC_DEV
        t = lax.rem(y - owner // NZ + ny, ny)
        j = lax.rem(z - lax.rem(owner, NZ) + NZ, NZ)
        return t * NZ + j, t, j, named - owner * DOC_DEV

    token = lax.broadcasted_iota(jnp.int32, (doc_len, 128), 0)

    def settle(p):
        for j in range(NZ):
            for t in range(1, ny):
                if relayed(t, j):
                    forward(p, j).wait_recv()
                else:
                    across(p, t, j).wait_recv()
        if p == KEY:
            for t in range(1, ny):
                pos_across(t).wait_recv()
            fetch[3].wait()

    def lay_out(p, r):
        every[p][r, context : context + tokens] = has["own"][
            r * tokens : (r + 1) * tokens, p * head_dim : (p + 1) * head_dim
        ]
        for k in range(slots):
            e = r * slots + k
            slot, t, j, local = slot_of(e)
            doc = ctx[p][slot]
            every[p][r, k * doc_len : (k + 1) * doc_len] = doc
            hot = (all_pos[t, j, pl.ds(local, 1)] == token).astype(jnp.bfloat16)
            rows_of = lax.dot_general(hot, doc, (((0,), (0,)), ((), ())), preferred_element_type=jnp.float32)
            dev[p, e * dev_tok : (e + 1) * dev_tok] = rows_of[:dev_tok]

    def renew(p, r, g, weights, total):
        first = r * slots + g * group
        rows = slice(first * dev_tok, (first + group) * dev_tok)
        known = (g + 1) * group * doc_len
        summed = jnp.dot(weights, every[p][r, :known], preferred_element_type=jnp.float32)
        delta = gain_ref[:, p * head_dim : (p + 1) * head_dim] * (summed / total)
        renewed = (dev[p, rows] + delta).astype(jnp.bfloat16)
        for i in range(group):
            fresh[p][first + i] = renewed[i * dev_tok : (i + 1) * dev_tok]
        return jnp.sum(delta * delta, axis=1, keepdims=True) * (0.5 / head_dim)

    def key_update(r, g):
        first = r * slots + g * group
        rows = slice(first * dev_tok, (first + group) * dev_tok)
        known = (g + 1) * group * doc_len
        scores = lax.dot_general(
            dev[KEY, rows].astype(jnp.bfloat16),
            every[KEY][r, :known],
            (((1,), (1,)), ((), ())),
            preferred_element_type=jnp.float32,
        )
        shape = (group * dev_tok, group * doc_len)
        row_slot = lax.broadcasted_iota(jnp.int32, shape, 0) // dev_tok
        key_slot = lax.broadcasted_iota(jnp.int32, shape, 1) // doc_len
        newest = jnp.where(row_slot >= key_slot, scores[:, known - shape[1] :], very_low)
        scores = newest if g == 0 else jnp.concatenate([scores[:, : known - shape[1]], newest], axis=1)
        top = jnp.max(scores, axis=1, keepdims=True)
        weights = jnp.exp2((scores - top) * (scale * LOG2E))
        total = jnp.sum(weights, axis=1, keepdims=True)
        weights = weights.astype(jnp.bfloat16)
        weights_of[g][r] = weights
        square = renew(KEY, r, g, weights, total)
        totals[rows] = jnp.broadcast_to(total, (group * dev_tok, 128))
        columns[rows] = jnp.broadcast_to(square, (group * dev_tok, 128))

    lane_slot = lax.broadcasted_iota(jnp.int32, (1, group * dev_tok), 1) // dev_tok

    def value_update(r, g):
        first = r * slots + g * group
        rows = slice(first * dev_tok, (first + group) * dev_tok)
        square = renew(VALUE, r, g, weights_of[g][r], totals[rows])
        both = (columns[rows] + square).T[:1]
        squares[r * GROUPS + g : r * GROUPS + g + 1, : group * dev_tok] = jnp.where(
            lane_slot + g * group < count_ref[me * REQ_DEV + r], both, 0.0
        )

    def back(p, s):
        return remote(upd[p].at[s], ret[p].at[me], has["send"].at[p, s], has["recv"].at[p, s], holder(s))

    def turn_aside(p, t):
        s = t * NZ + half
        way = 1 - 2 * (t % 2)
        sems = has["send"].at[p, s], has["trecv"].at[p, t]
        return remote(upd[p].at[s], turn_buf[p].at[t], *sems, place(ny, y, z + way))

    def turn_forward(p, t):
        way = 1 - 2 * (t % 2)
        sems = has["tsend"].at[p, t], has["recv"].at[p, t * NZ + half]
        target = place(ny, y - t, z - way - half)
        return remote(turn_buf[p].at[t], ret[p].at[place(ny, y, z - way)], *sems, target)

    def renewed_for(p, s):
        code = table_ref[peers + s]
        e = lax.rem(code // 8, 64)
        r = e // slots
        used = jnp.logical_and(code >= 512, e - r * slots < count_ref[me * REQ_DEV + r])
        return fresh[p][jnp.where(used, e, entries)]

    def far_first(i):
        k = i // ny
        j = jnp.where(lax.rem(k, 2) == 0, half - 1 - k // 2, half + 1 + k // 2)
        return lax.rem(i, ny) * NZ + j

    def give_back(p):
        for t in range(ny):
            upd[p][t * NZ + half] = renewed_for(p, t * NZ + half)
            turn_aside(p, t).start()

        def launch(i, carry):
            s = far_first(i)
            upd[p][s] = renewed_for(p, s)
            back(p, s).start()
            return carry

        lax.fori_loop(0, ny * (NZ - 2), launch, 0)
        for t in range(1, ny):
            upd[p][t * NZ] = renewed_for(p, t * NZ)
            back(p, t * NZ).start()
        ret[p][me] = renewed_for(p, 0)

    def turn(p):
        for t in range(ny):
            turn_aside(p, t).wait_recv()
            turn_forward(p, t).start()

    def share(k):
        return pltpu.make_async_remote_copy(
            src_ref=squares,
            dst_ref=parts.at[head_at],
            send_sem=has["hsend"].at[k],
            recv_sem=has["hrecv"].at[k],
            device_id={"heads": fellows[k]},
            device_id_type=MESH,
        )

    begin(KEY)
    for way in range(2):
        ring_of_pos(way, 1).start()
    pick(KEY, base[KEY], 0)
    travel(KEY, [])

    idle = lambda: None
    tasks = [lambda: arrive(KEY), lambda: pick(VALUE, base[VALUE], 0), idle]
    tasks += [lambda: settle(KEY)] + [functools.partial(lay_out, KEY, r) for r in range(REQ_DEV)]
    tasks += [functools.partial(key_update, r, g) for r in range(REQ_DEV) for g in range(GROUPS)]
    travel(VALUE, tasks)

    give_back(KEY)
    arrive(VALUE)
    settle(VALUE)
    turn(KEY)
    for r in range(REQ_DEV):
        lay_out(VALUE, r)
    for r in range(REQ_DEV):
        for g in range(GROUPS):
            value_update(r, g)
    give_back(VALUE)
    for k in range(1, nh):
        share(k).start()
    parts[head_at] = squares[...]

    fetch[2].wait()
    row = lax.broadcasted_iota(jnp.int32, (tokens, span - context), 0)
    col = lax.broadcasted_iota(jnp.int32, (tokens, span - context), 1)
    causal = row >= col
    place_of = lax.broadcasted_iota(jnp.int32, (1, context), 1)
    for r in range(REQ_DEV):
        live = place_of < count_ref[me * REQ_DEV + r] * doc_len

        def head(i, carry):
            cols = pl.ds(pl.multiple_of(i * head_dim, head_dim), head_dim)
            scores = lax.dot_general(
                has["q"][r * tokens : (r + 1) * tokens, cols],
                every[KEY][r],
                (((1,), (1,)), ((), ())),
                preferred_element_type=jnp.float32,
            )
            docs = jnp.where(live, scores[:, :context], very_low)
            own = jnp.where(causal, scores[:, context:], very_low)
            top = jnp.maximum(jnp.max(docs, axis=1, keepdims=True), jnp.max(own, axis=1, keepdims=True))
            docs = jnp.exp2((docs - top) * (scale * LOG2E))
            own = jnp.exp2((own - top) * (scale * LOG2E))
            total = jnp.sum(docs, axis=1, keepdims=True) + jnp.sum(own, axis=1, keepdims=True)
            summed = jnp.dot(
                docs.astype(jnp.bfloat16), every[VALUE][r, :context], preferred_element_type=jnp.float32
            ) + jnp.dot(own.astype(jnp.bfloat16), every[VALUE][r, context:], preferred_element_type=jnp.float32)
            att_ref[r * tokens : (r + 1) * tokens, cols] = (summed / total).astype(jnp.bfloat16)
            return carry

        if r == 0:
            lax.fori_loop(0, 1, head, 0)
            turn(VALUE)
            lax.fori_loop(1, heads, head, 0)
        else:
            lax.fori_loop(0, heads, head, 0)

    for k in range(1, nh):
        share(k).wait()
    total = parts[0]
    for k in range(1, nh):
        total = total + parts[k]
    sum_ref[...] = total * (1.0 / KVH)

    for p in range(2):
        for way in range(2):
            for step in range(1, half):
                for chunk in range(CHUNKS):
                    ring(p, way, step, chunk).wait_send()
        for t in range(ny):
            last_hop(p, t).wait_send()
        for j in range(NZ):
            for t in range(1, ny):
                across(p, t, j).wait_send()
            if j != half:
                forward(p, j).wait_send()
    for way in range(2):
        for step in range(1, half + 1 - way):
            ring_of_pos(way, step).wait_send()
    for t in range(1, ny):
        pos_across(t).wait_send()

    for p in range(2):

        def land(i, carry):
            back(p, far_first(i)).wait()
            return carry

        lax.fori_loop(0, ny * (NZ - 2), land, 0)
        for t in range(ny):
            if t:
                back(p, t * NZ).wait()
            turn_aside(p, t).wait_send()
            turn_forward(p, t).wait()


def blend(slots, table, lists, counts, cache, pos, gain, queries, own):
    peers = lax.axis_size("docs")
    ny = peers // NZ
    nh = lax.axis_size("heads")
    half = NZ // 2
    full = half - 1
    entries = REQ_DEV * slots
    dev_tok = pos.shape[1]
    doc_len, width = cache.shape[1:]
    head_dim = width // 2
    tokens = own.shape[0] // REQ_DEV
    span = slots * doc_len + (tokens + 127) // 128 * 128
    rows = slots // GROUPS * dev_tok
    doc = (doc_len, head_dim)
    packet = (dev_tok, head_dim)
    square = jax.ShapeDtypeStruct((REQ_DEV * GROUPS, 128), jnp.float32)
    bf16, f32 = jnp.bfloat16, jnp.float32
    scratch = {}
    for p in range(2):
        for name, shape in (
            ("base", (DOC_DEV,) + doc),
            ("far", (ny,) + doc),
            ("last", (ny,) + doc),
            ("picked", (ny, NZ) + doc),
            ("relay", (NZ,) + doc),
            ("ctx", (peers,) + doc),
            ("all", (REQ_DEV, span, head_dim)),
            ("fresh", (entries + 1,) + packet),
            ("upd", (peers,) + packet),
            ("turn", (ny,) + packet),
        ):
            scratch["%s%d" % (name, p)] = VMEM(shape, bf16)
        for way in range(2):
            for step in range(full):
                scratch["ring%d%d%d" % (p, way, step)] = VMEM((DOC_DEV,) + doc, bf16)
    for g in range(GROUPS):
        scratch["weights%d" % g] = VMEM((REQ_DEV, rows, (g + 1) * slots // GROUPS * doc_len), bf16)
    scratch["q"] = VMEM(queries.shape, bf16)
    scratch["own"] = VMEM(own.shape, bf16)
    scratch["dev"] = VMEM((2, entries * dev_tok, head_dim), f32)
    scratch["totals"] = VMEM((entries * dev_tok, 128), f32)
    scratch["columns"] = VMEM((entries * dev_tok, 128), f32)
    scratch["squares"] = VMEM(square.shape, f32)
    scratch["parts"] = VMEM((nh,) + square.shape, f32)
    scratch["ring_pos"] = VMEM((NZ, 8, 128), jnp.int32)
    scratch["all_pos"] = VMEM((ny, NZ, 8, 128), jnp.int32)
    for name, shape in (
        ("zsend", (2, 2, full, CHUNKS)), ("zrecv", (2, 2, full, CHUNKS)),
        ("lsend", (2, ny)), ("lrecv", (2, ny)),
        ("psend", (2, half + ny)), ("precv", (2, half + ny)),
        ("ysend", (2, ny, NZ)), ("yrecv", (2, ny, NZ)),
        ("fsend", (2, NZ)), ("frecv", (2, NZ)),
        ("send", (2, peers)), ("recv", (2, peers)),
        ("tsend", (2, ny)), ("trecv", (2, ny)),
        ("hsend", (nh,)), ("hrecv", (nh,)),
        ("local_sem", (4,)),
    ):
        scratch[name] = DMA(shape)
    any_space, vmem = whole(pl.ANY), whole(VMEM)
    return pl.pallas_call(
        functools.partial(blend_kernel, ny, nh, slots, dev_tok, tuple(scratch)),
        out_shape=(
            jax.ShapeDtypeStruct(queries.shape, bf16),
            jax.ShapeDtypeStruct((peers,) + packet, bf16),
            jax.ShapeDtypeStruct((peers,) + packet, bf16),
            square,
        ),
        in_specs=[whole(SMEM)] * 3 + [any_space, vmem, vmem, any_space, any_space],
        out_specs=(vmem,) * 4,
        scratch_shapes=list(scratch.values()),
        compiler_params=pltpu.CompilerParams(
            collective_id=0, has_side_effects=True, vmem_limit_bytes=56 * 2**20
        ),
        name="blend",
    )(table, lists, counts, cache, pos, gain, queries, own)


def shards(queries, own_kv, cache, doc_lists, doc_counts, dev_pos, blend_gain):
    width = blend_gain.shape[1]
    peers = lax.axis_size("docs")
    ny = peers // NZ
    me = lax.axis_index("docs")
    y, z = me // NZ, me % NZ
    slots = doc_lists.shape[1]
    dev_tok = dev_pos.shape[1]
    doc_len = cache.shape[0] // DOC_DEV

    lists = doc_lists.T
    owner = lists // DOC_DEV
    k = lax.broadcasted_iota(jnp.int32, lists.shape, 0)
    request = lax.broadcasted_iota(jnp.int32, lists.shape, 1)
    pair = request // REQ_DEV * peers + owner
    code = 512 + 8 * (request % REQ_DEV * slots + k) + lists - owner * DOC_DEV
    n = jnp.arange(2 * peers + 128, dtype=jnp.int32)
    t, j = n // NZ % ny, n % NZ
    picks = ((y + t) % ny * NZ + z) * peers + y * NZ + (z - j) % NZ
    returns = me * peers + (y - t) % ny * NZ + (z - j) % NZ
    way = jnp.where(j < ny // 2, 1, -1)
    last = ((y + j) % ny * NZ + (z + way) % NZ) * peers + y * NZ + (z - way * (NZ // 2 - 1)) % NZ
    want = jnp.where(n < peers, picks, jnp.where(n < 2 * peers, returns, last))
    table = jnp.sum(jnp.where(pair[None] == want[:, None, None], code[None], 0), axis=(1, 2))

    att, retk, retv, sums = blend(
        slots, table, lists, doc_counts, cache.reshape(DOC_DEV, doc_len, width), dev_pos, blend_gain, queries, own_kv
    )
    group_rows = slots // GROUPS * dev_tok
    dev_score = sums.reshape(REQ_DEV, GROUPS, 128)[:, :, :group_rows].reshape(REQ_DEV, slots, dev_tok)
    return att, jnp.concatenate([retk, retv], axis=2), dev_score


def solution(mesh):
    return jax.shard_map(
        shards,
        mesh=mesh,
        in_specs=(
            P("docs", "heads"),
            P("docs", "heads"),
            P("docs", "heads"),
            P(),
            P(),
            P("docs", None),
            P("heads", None),
        ),
        out_specs=(P("docs", "heads"), P("docs", None, "heads"), P("docs", None, None)),
        check_vma=False,
    )
```

time: 498 us -> 154 us (0.31)
  waiting for transfers between devices: 246 us -> 0 us
  Pallas kernels: 0 us -> 146 us
  starting transfers between devices: 71.1 us -> 0 us
  matrix products: 59.5 us -> 0 us
  local copies, waits for them, and re-layouts: 56.6 us -> 1.59 us
  loops' own time: 23.1 us -> 0 us
  other arithmetic: 26.6 us -> 3.89 us
  blocking collectives: 10.8 us -> 0 us
    all_to_all x3 -> x0, waiting for transfers between devices: 246 us -> none  [the longest x1 181 us: shards(): lax.all_to_all(send_blocks, 'docs', split_axis=0, concat_axis=0, tiled=True)]
    pallas_call x0 -> x1, Pallas kernels: none -> 146 us  [blend(): pl.pallas_call(functools.partial(blend_kernel, ny, nh, slots, dev_tok, tu...]
    all_to_all x3 -> x0, starting transfers between devices: 71.1 us -> none  [the longest x1 45.6 us: shards(): lax.all_to_all(outgoing.reshape(peers, capacity, dev_tok, local_heads * w...]
    dot_general x128 -> x0, matrix products: 59.5 us -> none  [the longest x31 19.7 us: slot_step(): jnp.dot(dev_rows[:, :head_dim], keys.T, preferred_element_type=jnp.float32)]
    squeeze x31 -> x0, local copies, waits for them, and re-layouts: 26.3 us -> none  [advance(): block = lax.dynamic_index_in_dim(context_head, slot, 0, keepdims=False)]
    another operation x2 -> x0, loops' own time: 23.1 us -> none  [shards(): state = lax.fori_loop(0, count, advance, state)]
    reduce_sum x67 -> x1, other arithmetic: 15.7 us -> 0.97 us  [shards(): jnp.sum(jnp.where(pair[None] == want[:, None, None], code[None], 0), axis...]
    gather x6 -> x0, local copies, waits for them, and re-layouts: 12.1 us -> none  [the longest x1 4.59 us: shards(): got_blocks.reshape(peers * capacity, doc_len, cache.shape[1])[slot_key]]
  transfers between devices with their start and end apart: 3 -> 0, of which waited for: 3 -> 0; matrix products, arithmetic and copies ran while one was open for 3% -> 0% of each run, Pallas kernels for 0% -> 0%
where the time goes in v4:
time: 154 us; the launch traced here: 152 us
  Pallas kernels  146 us (95%)
  other arithmetic  3.89 us (3%)
  local copies, waits for them, and re-layouts  1.59 us (1%)
    pallas_call x1, Pallas kernels, blend(): pl.pallas_call(functools.partial(blend_kernel, ny, nh, slots, dev_tok, tu...  146 us

profile of v4, /device:TPU:6, one launch (start us, length us, event | category | flops | bytes accessed | tf_op | source)
XLA Modules:
  0.0 152.0 jit_solution(10712489648878808311)
XLA Ops:
  0.7 0.7 multiply_add_fusion
  1.4 1.0 select_reduce_fusion.table_ref
  2.4 145.8 %blend.1 = (bf16[384,1024]{1,0:T(8,128)(2,1)}, bf16[64,24,128]{2,1,0:T(8,128)(2,1)}, bf16[64,24,128]{2,1,0:T(8,128)(2,1)}, f32[8,128]{1,0:T(8,128)}) custom-call(s32[256]{0:T(256)} %select_reduce_fusion.table_ref, s32[20,128]{1,0:T(8,128)} %bitcast.7, s32[128]{0:T(128)} %count_ref.1, bf16[6,128,256]{2,1,0:T(8,128)(2,1)} %bitcast.6, s32[6,24]{1,0:T(8,128)} %pos_ref.1, ...), custom_call_target="tpu_custom_call" | custom-call | tf_op jit(solution)/shard_map/blend/pallas_call | solution.py:508
  148.2 0.0 copy-start.1
  148.2 0.0 copy-start
  148.2 2.2 %pad_maximum_fusion = bf16[64,24,256]{2,1,0:T(8,128)(2,1)} fusion(bf16[64,24,128]{2,1,0:T(8,128)(2,1)} %get-tuple-element.9, bf16[64,24,128]{2,1,0:T(8,128)(2,1)} %get-tuple-element.8), kind=kLoop, calls=%fused_computation.1 | loop fusion | flops 1572864 | bytes 1572864 | tf_op jit(solution)/shard_map/concatenate | solution.py:556
  150.4 0.0 copy-done.1
  150.4 0.1 reshape.144
  150.5 0.6 copy.11
  151.1 0.0 copy-done
  151.1 0.9 copy.13
  (4 shorter events, 0.0 us)
Async XLA Ops:
  148.2 2.2 %copy-start.1 = (f32[8,128]{1,0:T(8,128)S(1)}, f32[8,128]{1,0:T(8,128)}, u32[]{:S(2)}) copy-start(f32[8,128]{1,0:T(8,128)} %get-tuple-element.10) | copy-start | bytes 12292
  148.2 2.9 %copy-start = (bf16[384,1024]{1,0:T(8,128)(2,1)S(1)}, bf16[384,1024]{1,0:T(8,128)(2,1)}, u32[]{:S(2)}) copy-start(bf16[384,1024]{1,0:T(8,128)(2,1)} %get-tuple-element.28) | copy-start | bytes 2359300

commit v5 on v4

--- a/solution.py
+++ b/solution.py
@@ -18,7 +18,8 @@
 MESH = pl.DeviceIdType.MESH
 LOG2E = 1.4426950408889634
 GROUPS = 4
-CHUNKS = 3
+LEAD = 3
+CHUNKS = 2
 KEY, VALUE = 0, 1
 
 
@@ -32,7 +33,7 @@
 
 def blend_kernel(
     ny, nh, slots, dev_tok, names, table_ref, list_ref, count_ref, cache_ref, pos_ref, gain_ref, q_ref, own_ref,
-    att_ref, retk_ref, retv_ref, sum_ref, *scratch
+    att_ref, ret_ref, sum_ref, *scratch
 ):
     has = dict(zip(names, scratch))
     peers = ny * NZ
@@ -51,14 +52,13 @@
     y, z = me // NZ, lax.rem(me, NZ)
     head_at = lax.axis_index("heads")
     fellows = [lax.rem(head_at + k, nh) for k in range(nh)]
-    ret = (retk_ref, retv_ref)
     local_sem = has["local_sem"]
 
     def two(name):
         return has[name + "0"], has[name + "1"]
 
-    base, far, last_pick, picked, relay, ctx, every, fresh, upd, turn_buf = map(
-        two, ("base", "far", "last", "picked", "relay", "ctx", "all", "fresh", "upd", "turn")
+    base, far, last_pick, picked, ctx, every, fresh, upd, turn_buf = map(
+        two, ("base", "far", "last", "picked", "ctx", "all", "fresh", "upd", "turn")
     )
     passing = [[[has["ring%d%d%d" % (p, way, s)] for s in range(full)] for way in range(2)] for p in range(2)]
     ring_pos, all_pos, dev, squares, parts = (has[n] for n in ("ring_pos", "all_pos", "dev", "squares", "parts"))
@@ -92,7 +92,8 @@
     squares[...] = jnp.zeros_like(squares)
     for p in range(2):
         fresh[p][entries] = jnp.zeros(fresh[p].shape[1:], fresh[p].dtype)
-        every[p][...] = jnp.zeros_like(every[p])
+        every[p][:, context:, :head_dim] = jnp.zeros((REQ_DEV, span - context, head_dim), jnp.bfloat16)
+    every[VALUE][:, :, head_dim:] = jnp.ones((REQ_DEV, span, head_dim), jnp.bfloat16)
     fetch[KEY].wait()
     pl.semaphore_wait(barrier, peers + nh - 2)
 
@@ -124,29 +125,10 @@
         sems = has["psend"].at[0, half + t], has["precv"].at[0, half + t]
         return remote(ring_pos, all_pos.at[t], *sems, along_y[t])
 
-    def aside(j):
-        return along_y[1] if j % 2 == 0 else along_y[ny - 1]
-
-    def relayed(t, j):
-        return 2 * t == ny and j != half
-
     def across(p, t, j):
         src = far[p].at[t] if j == half else picked[p].at[t, j]
-        dst = relay[p].at[j] if relayed(t, j) else ctx[p].at[t * NZ + j]
-        recv = has["frecv"].at[p, j] if relayed(t, j) else has["yrecv"].at[p, t, j]
-        return remote(src, dst, has["ysend"].at[p, t, j], recv, aside(j) if relayed(t, j) else along_y[t])
-
-    def forward(p, j):
-        sems = has["fsend"].at[p, j], has["yrecv"].at[p, ny // 2, j]
-        return remote(relay[p].at[j], ctx[p].at[ny // 2 * NZ + j], *sems, aside(j))
-
-    waiting = []
-
-    def pass_on():
-        for p, j in waiting:
-            across(p, ny // 2, j).wait_recv()
-            forward(p, j).start()
-        waiting.clear()
+        sems = has["ysend"].at[p, t, j], has["yrecv"].at[p, t, j]
+        return remote(src, ctx[p].at[t * NZ + j], *sems, along_y[t])
 
     def pick(p, buf, j):
         for t in [ny // 2] + [t for t in range(1, ny) if 2 * t != ny] + [0]:
@@ -156,48 +138,38 @@
                 across(p, t, j).start()
             else:
                 ctx[p][j] = doc
-        waiting.append((p, j))
 
     def begin(p):
         for chunk in range(CHUNKS):
             for way in range(2):
                 ring(p, way, 1, chunk).start()
 
-    def travel(p, tasks):
-        todo = list(tasks)
-        for step in range(1, half):
-            for chunk in range(CHUNKS):
+    def hop(p, step, todo):
+        for chunk in range(CHUNKS):
+            for way in range(2):
+                ring(p, way, step, chunk).wait_recv()
+                if step < full:
+                    ring(p, way, step + 1, chunk).start()
+            if p == KEY and chunk == 0:
                 for way in range(2):
-                    ring(p, way, step, chunk).wait_recv()
-                    if step < full:
-                        ring(p, way, step + 1, chunk).start()
-                if p == KEY and chunk == 0:
-                    for way in range(2):
-                        ring_of_pos(way, step).wait_recv()
-                        if way == 0 or step < full:
-                            ring_of_pos(way, step + 1).start()
-                if chunk < CHUNKS - 1 and todo:
-                    todo.pop(0)()
-            if step == full:
-                for t in range(ny):
-                    buf = passing[p][2 * t // ny][full - 1]
-                    last_pick[p][t] = buf[lax.rem(table_ref[2 * peers + t], 8)]
-                    last_hop(p, t).start()
-                if p == KEY:
-                    fetch[VALUE].wait()
-                    begin(VALUE)
-            pass_on()
-            pick(p, passing[p][0][step - 1], step)
-            pick(p, passing[p][1][step - 1], NZ - step)
-            if todo:
+                    ring_of_pos(way, step).wait_recv()
+                    if way == 0 or step < full:
+                        ring_of_pos(way, step + 1).start()
+            if chunk < CHUNKS - 1 and todo:
                 todo.pop(0)()
-        for task in todo:
-            task()
+        if step == full:
+            for t in range(ny):
+                buf = passing[p][2 * t // ny][full - 1]
+                last_pick[p][t] = buf[lax.rem(table_ref[2 * peers + t], 8)]
+                last_hop(p, t).start()
+        pick(p, passing[p][0][step - 1], step)
+        pick(p, passing[p][1][step - 1], NZ - step)
+        if todo:
+            todo.pop(0)()
 
     def arrive(p):
         for t in range(ny):
             last_hop(p, t).wait_recv()
-        pass_on()
         for t in range(1, ny):
             across(p, t, half).start()
         ctx[p][half] = far[p][0]
@@ -219,24 +191,21 @@
     def settle(p):
         for j in range(NZ):
             for t in range(1, ny):
-                if relayed(t, j):
-                    forward(p, j).wait_recv()
-                else:
-                    across(p, t, j).wait_recv()
+                across(p, t, j).wait_recv()
         if p == KEY:
             for t in range(1, ny):
                 pos_across(t).wait_recv()
             fetch[3].wait()
 
     def lay_out(p, r):
-        every[p][r, context : context + tokens] = has["own"][
+        every[p][r, context : context + tokens, :head_dim] = has["own"][
             r * tokens : (r + 1) * tokens, p * head_dim : (p + 1) * head_dim
         ]
         for k in range(slots):
             e = r * slots + k
             slot, t, j, local = slot_of(e)
             doc = ctx[p][slot]
-            every[p][r, k * doc_len : (k + 1) * doc_len] = doc
+            every[p][r, k * doc_len : (k + 1) * doc_len, :head_dim] = doc
             hot = (all_pos[t, j, pl.ds(local, 1)] == token).astype(jnp.bfloat16)
             rows_of = lax.dot_general(hot, doc, (((0,), (0,)), ((), ())), preferred_element_type=jnp.float32)
             dev[p, e * dev_tok : (e + 1) * dev_tok] = rows_of[:dev_tok]
@@ -245,7 +214,7 @@
         first = r * slots + g * group
         rows = slice(first * dev_tok, (first + group) * dev_tok)
         known = (g + 1) * group * doc_len
-        summed = jnp.dot(weights, every[p][r, :known], preferred_element_type=jnp.float32)
+        summed = jnp.dot(weights, every[p][r, :known, :head_dim], preferred_element_type=jnp.float32)
         delta = gain_ref[:, p * head_dim : (p + 1) * head_dim] * (summed / total)
         renewed = (dev[p, rows] + delta).astype(jnp.bfloat16)
         for i in range(group):
@@ -287,8 +256,11 @@
             lane_slot + g * group < count_ref[me * REQ_DEV + r], both, 0.0
         )
 
+    def ret_part(p, home):
+        return ret_ref.at[home, :, pl.ds(p * head_dim, head_dim)]
+
     def back(p, s):
-        return remote(upd[p].at[s], ret[p].at[me], has["send"].at[p, s], has["recv"].at[p, s], holder(s))
+        return remote(upd[p].at[s], ret_part(p, me), has["send"].at[p, s], has["recv"].at[p, s], holder(s))
 
     def turn_aside(p, t):
         s = t * NZ + half
@@ -300,7 +272,7 @@
         way = 1 - 2 * (t % 2)
         sems = has["tsend"].at[p, t], has["recv"].at[p, t * NZ + half]
         target = place(ny, y - t, z - way - half)
-        return remote(turn_buf[p].at[t], ret[p].at[place(ny, y, z - way)], *sems, target)
+        return remote(turn_buf[p].at[t], ret_part(p, place(ny, y, z - way)), *sems, target)
 
     def renewed_for(p, s):
         code = table_ref[peers + s]
@@ -329,7 +301,7 @@
         for t in range(1, ny):
             upd[p][t * NZ] = renewed_for(p, t * NZ)
             back(p, t * NZ).start()
-        ret[p][me] = renewed_for(p, 0)
+        ret_ref[me, :, p * head_dim : (p + 1) * head_dim] = renewed_for(p, 0)
 
     def turn(p):
         for t in range(ny):
@@ -350,13 +322,28 @@
     for way in range(2):
         ring_of_pos(way, 1).start()
     pick(KEY, base[KEY], 0)
-    travel(KEY, [])
-
-    idle = lambda: None
-    tasks = [lambda: arrive(KEY), lambda: pick(VALUE, base[VALUE], 0), idle]
-    tasks += [lambda: settle(KEY)] + [functools.partial(lay_out, KEY, r) for r in range(REQ_DEV)]
+    tasks = [lambda: arrive(KEY), lambda: settle(KEY)]
+    tasks += [functools.partial(lay_out, KEY, r) for r in range(REQ_DEV)]
     tasks += [functools.partial(key_update, r, g) for r in range(REQ_DEV) for g in range(GROUPS)]
-    travel(VALUE, tasks)
+    lead = min(LEAD, full)
+    for tick in range(1, full + lead + 1):
+        if tick <= full:
+            hop(KEY, tick, [])
+        if tick == lead:
+            fetch[VALUE].wait()
+            begin(VALUE)
+            pick(VALUE, base[VALUE], 0)
+        if tick > lead:
+            todo = []
+            if tick > full:
+                share_of = -(-len(tasks) // (full + lead + 1 - tick))
+                turns, tasks = tasks[:share_of], tasks[share_of:]
+                middle = len(turns) // 2
+                todo = [
+                    functools.partial(lambda some: [one() for one in some], turns[:middle]),
+                    functools.partial(lambda some: [one() for one in some], turns[middle:]),
+                ]
+            hop(VALUE, tick - lead, todo)
 
     give_back(KEY)
     arrive(VALUE)
@@ -377,35 +364,49 @@
     col = lax.broadcasted_iota(jnp.int32, (tokens, span - context), 1)
     causal = row >= col
     place_of = lax.broadcasted_iota(jnp.int32, (1, context), 1)
-    for r in range(REQ_DEV):
-        live = place_of < count_ref[me * REQ_DEV + r] * doc_len
-
-        def head(i, carry):
-            cols = pl.ds(pl.multiple_of(i * head_dim, head_dim), head_dim)
-            scores = lax.dot_general(
-                has["q"][r * tokens : (r + 1) * tokens, cols],
-                every[KEY][r],
-                (((1,), (1,)), ((), ())),
-                preferred_element_type=jnp.float32,
-            )
-            docs = jnp.where(live, scores[:, :context], very_low)
-            own = jnp.where(causal, scores[:, context:], very_low)
-            top = jnp.maximum(jnp.max(docs, axis=1, keepdims=True), jnp.max(own, axis=1, keepdims=True))
-            docs = jnp.exp2((docs - top) * (scale * LOG2E))
-            own = jnp.exp2((own - top) * (scale * LOG2E))
-            total = jnp.sum(docs, axis=1, keepdims=True) + jnp.sum(own, axis=1, keepdims=True)
-            summed = jnp.dot(
-                docs.astype(jnp.bfloat16), every[VALUE][r, :context], preferred_element_type=jnp.float32
-            ) + jnp.dot(own.astype(jnp.bfloat16), every[VALUE][r, context:], preferred_element_type=jnp.float32)
-            att_ref[r * tokens : (r + 1) * tokens, cols] = (summed / total).astype(jnp.bfloat16)
-            return carry
-
-        if r == 0:
-            lax.fori_loop(0, 1, head, 0)
-            turn(VALUE)
-            lax.fori_loop(1, heads, head, 0)
-        else:
-            lax.fori_loop(0, heads, head, 0)
+
+    def spot(n):
+        n = jnp.clip(n, 0, REQ_DEV * heads - 1)
+        r = n // heads
+        rows = pl.ds(pl.multiple_of(r * tokens, 16), tokens)
+        return r, rows, pl.ds(pl.multiple_of(lax.rem(n, heads) * head_dim, head_dim), head_dim)
+
+    def scores_of(n, out):
+        r, rows, cols = spot(n)
+        out[...] = lax.dot_general(
+            has["q"][rows, cols], every[KEY][r], (((1,), (1,)), ((), ())), preferred_element_type=jnp.float32
+        )
+
+    def weights_from(n, scores, out):
+        r, _, _ = spot(n)
+        docs = jnp.where(place_of < count_ref[me * REQ_DEV + r] * doc_len, scores[:, :context], very_low)
+        own = jnp.where(causal, scores[:, context:], very_low)
+        top = jnp.maximum(jnp.max(docs, axis=1, keepdims=True), jnp.max(own, axis=1, keepdims=True))
+        out[:, :context] = jnp.exp2((docs - top) * (scale * LOG2E)).astype(jnp.bfloat16)
+        out[:, context:] = jnp.exp2((own - top) * (scale * LOG2E)).astype(jnp.bfloat16)
+
+    def output_of(n, weights):
+        r, rows, cols = spot(n)
+        summed = jnp.dot(weights[...], every[VALUE][r], preferred_element_type=jnp.float32)
+        att_ref[rows, cols] = (summed[:, :head_dim] / summed[:, head_dim:]).astype(jnp.bfloat16)
+
+    score_a, score_b, weight_a, weight_b = (has[n] for n in ("score0", "score1", "weight0", "weight1"))
+
+    def pair(m, carry):
+        scores_of(2 * m + 1, score_b)
+        weights_from(2 * m, score_a, weight_a)
+        output_of(2 * m - 1, weight_b)
+        scores_of(2 * m + 2, score_a)
+        weights_from(2 * m + 1, score_b, weight_b)
+        output_of(2 * m, weight_a)
+        return carry
+
+    weight_b[...] = jnp.ones_like(weight_b)
+    scores_of(0, score_a)
+    lax.fori_loop(0, 1, pair, 0)
+    turn(VALUE)
+    lax.fori_loop(1, REQ_DEV * heads // 2, pair, 0)
+    output_of(REQ_DEV * heads - 1, weight_b)
 
     for k in range(1, nh):
         share(k).wait()
@@ -424,8 +425,6 @@
         for j in range(NZ):
             for t in range(1, ny):
                 across(p, t, j).wait_send()
-            if j != half:
-                forward(p, j).wait_send()
     for way in range(2):
         for step in range(1, half + 1 - way):
             ring_of_pos(way, step).wait_send()
@@ -470,9 +469,8 @@
             ("far", (ny,) + doc),
             ("last", (ny,) + doc),
             ("picked", (ny, NZ) + doc),
-            ("relay", (NZ,) + doc),
             ("ctx", (peers,) + doc),
-            ("all", (REQ_DEV, span, head_dim)),
+            ("all", (REQ_DEV, span, head_dim * (1 + p))),
             ("fresh", (entries + 1,) + packet),
             ("upd", (peers,) + packet),
             ("turn", (ny,) + packet),
@@ -483,6 +481,9 @@
                 scratch["ring%d%d%d" % (p, way, step)] = VMEM((DOC_DEV,) + doc, bf16)
     for g in range(GROUPS):
         scratch["weights%d" % g] = VMEM((REQ_DEV, rows, (g + 1) * slots // GROUPS * doc_len), bf16)
+    for name in ("0", "1"):
+        scratch["score" + name] = VMEM((tokens, span), f32)
+        scratch["weight" + name] = VMEM((tokens, span), bf16)
     scratch["q"] = VMEM(queries.shape, bf16)
     scratch["own"] = VMEM(own.shape, bf16)
     scratch["dev"] = VMEM((2, entries * dev_tok, head_dim), f32)
@@ -497,7 +498,6 @@
         ("lsend", (2, ny)), ("lrecv", (2, ny)),
         ("psend", (2, half + ny)), ("precv", (2, half + ny)),
         ("ysend", (2, ny, NZ)), ("yrecv", (2, ny, NZ)),
-        ("fsend", (2, NZ)), ("frecv", (2, NZ)),
         ("send", (2, peers)), ("recv", (2, peers)),
         ("tsend", (2, ny)), ("trecv", (2, ny)),
         ("hsend", (nh,)), ("hrecv", (nh,)),
@@ -509,12 +509,11 @@
         functools.partial(blend_kernel, ny, nh, slots, dev_tok, tuple(scratch)),
         out_shape=(
             jax.ShapeDtypeStruct(queries.shape, bf16),
-            jax.ShapeDtypeStruct((peers,) + packet, bf16),
-            jax.ShapeDtypeStruct((peers,) + packet, bf16),
+            jax.ShapeDtypeStruct((peers, dev_tok, width), bf16),
             square,
         ),
         in_specs=[whole(SMEM)] * 3 + [any_space, vmem, vmem, any_space, any_space],
-        out_specs=(vmem,) * 4,
+        out_specs=(vmem,) * 3,
         scratch_shapes=list(scratch.values()),
         compiler_params=pltpu.CompilerParams(
             collective_id=0, has_side_effects=True, vmem_limit_bytes=56 * 2**20
@@ -548,12 +547,12 @@
     want = jnp.where(n < peers, picks, jnp.where(n < 2 * peers, returns, last))
     table = jnp.sum(jnp.where(pair[None] == want[:, None, None], code[None], 0), axis=(1, 2))
 
-    att, retk, retv, sums = blend(
+    att, returned, sums = blend(
         slots, table, lists, doc_counts, cache.reshape(DOC_DEV, doc_len, width), dev_pos, blend_gain, queries, own_kv
     )
     group_rows = slots // GROUPS * dev_tok
     dev_score = sums.reshape(REQ_DEV, GROUPS, 128)[:, :, :group_rows].reshape(REQ_DEV, slots, dev_tok)
-    return att, jnp.concatenate([retk, retv], axis=2), dev_score
+    return att, returned, dev_score
 
 
 def solution(mesh):

time: 154 us -> 148 us (0.961)
  the two profiles are of different devices: /device:TPU:6 before, /device:TPU:24 now
where the time goes in v5:
time: 148 us
  Pallas kernels  141 us (95%)
  local copies, waits for them, and re-layouts  4.39 us (3%)
  other arithmetic  1.73 us (1%)
    pallas_call x1, Pallas kernels, blend(): pl.pallas_call(functools.partial(blend_kernel, ny, nh, slots, dev_tok, tu...  141 us
    unnamed x5, local copies, waits for them, and re-layouts  3.64 us

profile of v5, /device:TPU:24, one launch (start us, length us, event | category | flops | bytes accessed | tf_op | source)
XLA Modules:
  0.0 148.0 jit_solution(432143981804746007)
XLA Ops:
  0.7 0.7 multiply_add_fusion
  1.4 1.0 select_reduce_fusion.table_ref
  2.4 141.2 %blend.1 = (bf16[384,1024]{1,0:T(8,128)(2,1)}, bf16[64,24,256]{2,1,0:T(8,128)(2,1)}, f32[8,128]{1,0:T(8,128)}) custom-call(s32[256]{0:T(256)} %select_reduce_fusion.table_ref, s32[20,128]{1,0:T(8,128)} %bitcast.7, s32[128]{0:T(128)} %count_ref.1, bf16[6,128,256]{2,1,0:T(8,128)(2,1)} %bitcast.6, s32[6,24]{1,0:T(8,128)} %pos_ref.1, f32[1,256]{1,0:T(1,128)} %gain_ref.1, ...), custom_call_target="tpu_custom_call" | custom-call | tf_op jit(solution)/shard_map/blend/pallas_call | solution.py:508
  143.6 0.8 reshape.144
  144.3 0.6 copy.11
  144.9 0.0 copy-start
  144.9 2.1 %copy.14 = bf16[384,1024]{1,0:T(8,128)(2,1)} copy(bf16[384,1024]{1,0:T(8,128)(2,1)} %get-tuple-element.26) | data formatting | bytes 1572864
  147.1 0.0 copy-done
  147.1 0.9 copy.15
  (4 shorter events, 0.0 us)
Async XLA Ops:
  144.9 2.1 %copy-start = (bf16[64,24,256]{2,1,0:T(8,128)(2,1)S(1)}, bf16[64,24,256]{2,1,0:T(8,128)(2,1)}, u32[]{:S(2)}) copy-start(bf16[64,24,256]{2,1,0:T(8,128)(2,1)} %get-tuple-element.27) | copy-start | bytes 2359300

commit v6 on v5

--- a/solution.py
+++ b/solution.py
@@ -18,8 +18,9 @@
 MESH = pl.DeviceIdType.MESH
 LOG2E = 1.4426950408889634
 GROUPS = 4
-LEAD = 3
+LEAD = 4
 CHUNKS = 2
+EARLY = 4
 KEY, VALUE = 0, 1
 
 
@@ -57,8 +58,8 @@
     def two(name):
         return has[name + "0"], has[name + "1"]
 
-    base, far, last_pick, picked, ctx, every, fresh, upd, turn_buf = map(
-        two, ("base", "far", "last", "picked", "ctx", "all", "fresh", "upd", "turn")
+    base, far, last_pick, picked, ctx, every, fresh, upd, turn_buf, mid = map(
+        two, ("base", "far", "last", "picked", "ctx", "all", "fresh", "upd", "turn", "mid")
     )
     passing = [[[has["ring%d%d%d" % (p, way, s)] for s in range(full)] for way in range(2)] for p in range(2)]
     ring_pos, all_pos, dev, squares, parts = (has[n] for n in ("ring_pos", "all_pos", "dev", "squares", "parts"))
@@ -77,14 +78,13 @@
         one.start()
     barrier = pltpu.get_barrier_semaphore()
 
-    def holder(s):
-        return place(ny, y - s // NZ, z - lax.rem(s, NZ))
-
-    def greet(s, carry):
-        pl.semaphore_signal(barrier, inc=1, device_id={"docs": holder(s)}, device_id_type=MESH)
+    def greet(j, carry):
+        pl.semaphore_signal(barrier, inc=1, device_id={"docs": place(ny, y, z - j)}, device_id_type=MESH)
         return carry
 
-    lax.fori_loop(1, peers, greet, 0)
+    lax.fori_loop(1, NZ, greet, 0)
+    for t in range(1, ny):
+        pl.semaphore_signal(barrier, inc=1, device_id={"docs": place(ny, y + t, z)}, device_id_type=MESH)
     for k in range(1, nh):
         pl.semaphore_signal(barrier, inc=1, device_id={"heads": fellows[k]}, device_id_type=MESH)
     ring_pos[0] = jnp.full(ring_pos.shape[1:], -1, jnp.int32)
@@ -95,7 +95,7 @@
         every[p][:, context:, :head_dim] = jnp.zeros((REQ_DEV, span - context, head_dim), jnp.bfloat16)
     every[VALUE][:, :, head_dim:] = jnp.ones((REQ_DEV, span, head_dim), jnp.bfloat16)
     fetch[KEY].wait()
-    pl.semaphore_wait(barrier, peers + nh - 2)
+    pl.semaphore_wait(barrier, NZ - 1 + ny - 1 + nh - 1)
 
     along_z = [place(ny, y, z + 1), place(ny, y, z - 1)]
     along_y = [place(ny, y + t, z) for t in range(ny)]
@@ -125,19 +125,24 @@
         sems = has["psend"].at[0, half + t], has["precv"].at[0, half + t]
         return remote(ring_pos, all_pos.at[t], *sems, along_y[t])
 
-    def across(p, t, j):
-        src = far[p].at[t] if j == half else picked[p].at[t, j]
-        sems = has["ysend"].at[p, t, j], has["yrecv"].at[p, t, j]
-        return remote(src, ctx[p].at[t * NZ + j], *sems, along_y[t])
-
-    def pick(p, buf, j):
-        for t in [ny // 2] + [t for t in range(1, ny) if 2 * t != ny] + [0]:
-            doc = buf[lax.rem(table_ref[t * NZ + j], 8)]
+    def across(p, t, step):
+        at = pl.ds(1 if step == half else 2 * step, 1 if step in (0, half) else 2)
+        src = far[p].at[pl.ds(t, 1)] if step == half else picked[p].at[t, at]
+        sems = has["ysend"].at[p, t, step], has["yrecv"].at[p, t, step]
+        return remote(src, ctx[p].at[t, at], *sems, along_y[t])
+
+    def pick(p, step):
+        for t in list(range(1, ny)) + [0]:
+            for way in range(1 if step == 0 else 2):
+                buf = base[p] if step == 0 else passing[p][way][step - 1]
+                j = step if way == 0 else NZ - step
+                doc = buf[lax.rem(table_ref[t * NZ + j], 8)]
+                if t:
+                    picked[p][t, 2 * step + way] = doc
+                else:
+                    ctx[p][0, 2 * step + way] = doc
             if t:
-                picked[p][t, j] = doc
-                across(p, t, j).start()
-            else:
-                ctx[p][j] = doc
+                across(p, t, step).start()
 
     def begin(p):
         for chunk in range(CHUNKS):
@@ -162,8 +167,7 @@
                 buf = passing[p][2 * t // ny][full - 1]
                 last_pick[p][t] = buf[lax.rem(table_ref[2 * peers + t], 8)]
                 last_hop(p, t).start()
-        pick(p, passing[p][0][step - 1], step)
-        pick(p, passing[p][1][step - 1], NZ - step)
+        pick(p, step)
         if todo:
             todo.pop(0)()
 
@@ -172,7 +176,7 @@
             last_hop(p, t).wait_recv()
         for t in range(1, ny):
             across(p, t, half).start()
-        ctx[p][half] = far[p][0]
+        ctx[p][0, 1] = far[p][0]
         if p == KEY:
             ring_of_pos(0, half).wait_recv()
             for t in range(1, ny):
@@ -184,14 +188,15 @@
         owner = named // DOC_DEV
         t = lax.rem(y - owner // NZ + ny, ny)
         j = lax.rem(z - lax.rem(owner, NZ) + NZ, NZ)
-        return t * NZ + j, t, j, named - owner * DOC_DEV
+        at = jnp.where(j < half, 2 * j, 2 * (NZ - j) + 1)
+        return t, jnp.where(j == half, 1, at), j, named - owner * DOC_DEV
 
     token = lax.broadcasted_iota(jnp.int32, (doc_len, 128), 0)
 
     def settle(p):
-        for j in range(NZ):
+        for step in range(half + 1):
             for t in range(1, ny):
-                across(p, t, j).wait_recv()
+                across(p, t, step).wait_recv()
         if p == KEY:
             for t in range(1, ny):
                 pos_across(t).wait_recv()
@@ -203,8 +208,8 @@
         ]
         for k in range(slots):
             e = r * slots + k
-            slot, t, j, local = slot_of(e)
-            doc = ctx[p][slot]
+            t, at, j, local = slot_of(e)
+            doc = ctx[p][t, at]
             every[p][r, k * doc_len : (k + 1) * doc_len, :head_dim] = doc
             hot = (all_pos[t, j, pl.ds(local, 1)] == token).astype(jnp.bfloat16)
             rows_of = lax.dot_general(hot, doc, (((0,), (0,)), ((), ())), preferred_element_type=jnp.float32)
@@ -256,57 +261,71 @@
             lane_slot + g * group < count_ref[me * REQ_DEV + r], both, 0.0
         )
 
-    def ret_part(p, home):
-        return ret_ref.at[home, :, pl.ds(p * head_dim, head_dim)]
-
-    def back(p, s):
-        return remote(upd[p].at[s], ret_part(p, me), has["send"].at[p, s], has["recv"].at[p, s], holder(s))
-
-    def turn_aside(p, t):
-        s = t * NZ + half
-        way = 1 - 2 * (t % 2)
-        sems = has["send"].at[p, s], has["trecv"].at[p, t]
-        return remote(upd[p].at[s], turn_buf[p].at[t], *sems, place(ny, y, z + way))
-
-    def turn_forward(p, t):
-        way = 1 - 2 * (t % 2)
-        sems = has["tsend"].at[p, t], has["recv"].at[p, t * NZ + half]
-        target = place(ny, y - t, z - way - half)
-        return remote(turn_buf[p].at[t], ret_part(p, place(ny, y, z - way)), *sems, target)
-
-    def renewed_for(p, s):
-        code = table_ref[peers + s]
+    side = ny // 2
+
+    def back(p, j):
+        return remote(
+            upd[p].at[j], mid[p].at[:, z], has["send"].at[p, j], has["recv"].at[p, j], place(ny, y, z - j)
+        )
+
+    def turn_aside(p, w):
+        src = upd[p].at[half, pl.ds(w * side, side)]
+        sems = has["send"].at[p, NZ + w], has["trecv"].at[p, w]
+        return remote(src, turn_buf[p].at[w], *sems, along_z[w])
+
+    def turn_forward(p, w):
+        origin = lax.rem(z + NZ - 1 + 2 * w, NZ)
+        dst = mid[p].at[pl.ds(w * side, side), origin]
+        sems = has["tsend"].at[p, w], has["recv"].at[p, NZ + w]
+        return remote(turn_buf[p].at[w], dst, *sems, place(ny, y, origin - half))
+
+    def spread(p, u):
+        dst = ret_ref.at[pl.ds(y * NZ, NZ), :, pl.ds(p * head_dim, head_dim)]
+        return remote(mid[p].at[u], dst, has["gsend"].at[p, u], has["grecv"].at[p, u], along_y[u])
+
+    def renewed_for(p, u, j):
+        code = table_ref[peers + (ny - u) % ny * NZ + j]
         e = lax.rem(code // 8, 64)
         r = e // slots
         used = jnp.logical_and(code >= 512, e - r * slots < count_ref[me * REQ_DEV + r])
         return fresh[p][jnp.where(used, e, entries)]
 
     def far_first(i):
-        k = i // ny
-        j = jnp.where(lax.rem(k, 2) == 0, half - 1 - k // 2, half + 1 + k // 2)
-        return lax.rem(i, ny) * NZ + j
+        return jnp.where(lax.rem(i, 2) == 0, half - 1 - i // 2, half + 1 + i // 2)
 
     def give_back(p):
-        for t in range(ny):
-            upd[p][t * NZ + half] = renewed_for(p, t * NZ + half)
-            turn_aside(p, t).start()
+        for u in range(ny):
+            upd[p][half, u] = renewed_for(p, u, half)
+        for w in range(2):
+            turn_aside(p, w).start()
 
         def launch(i, carry):
-            s = far_first(i)
-            upd[p][s] = renewed_for(p, s)
-            back(p, s).start()
+            j = far_first(i)
+            for u in range(ny):
+                upd[p][j, u] = renewed_for(p, u, j)
+            back(p, j).start()
             return carry
 
-        lax.fori_loop(0, ny * (NZ - 2), launch, 0)
-        for t in range(1, ny):
-            upd[p][t * NZ] = renewed_for(p, t * NZ)
-            back(p, t * NZ).start()
-        ret_ref[me, :, p * head_dim : (p + 1) * head_dim] = renewed_for(p, 0)
+        lax.fori_loop(0, NZ - 2, launch, 0)
+        for u in range(ny):
+            mid[p][u, z] = renewed_for(p, u, 0)
 
     def turn(p):
-        for t in range(ny):
-            turn_aside(p, t).wait_recv()
-            turn_forward(p, t).start()
+        for w in range(2):
+            turn_aside(p, w).wait_recv()
+            turn_forward(p, w).start()
+
+    def spread_all(p):
+        def land(i, carry):
+            back(p, far_first(i)).wait_recv()
+            return carry
+
+        lax.fori_loop(0, NZ - 2, land, 0)
+        for w in range(2):
+            turn_forward(p, w).wait_recv()
+        for u in range(1, ny):
+            spread(p, u).start()
+        ret_ref[pl.ds(y * NZ, NZ), :, p * head_dim : (p + 1) * head_dim] = mid[p][0]
 
     def share(k):
         return pltpu.make_async_remote_copy(
@@ -318,13 +337,62 @@
             device_id_type=MESH,
         )
 
+    row = lax.broadcasted_iota(jnp.int32, (tokens, span - context), 0)
+    col = lax.broadcasted_iota(jnp.int32, (tokens, span - context), 1)
+    causal = row >= col
+    place_of = lax.broadcasted_iota(jnp.int32, (1, context), 1)
+
+    def spot(n):
+        n = jnp.clip(n, 0, REQ_DEV * heads - 1)
+        r = n // heads
+        rows = pl.ds(pl.multiple_of(r * tokens, 16), tokens)
+        return r, rows, pl.ds(pl.multiple_of(lax.rem(n, heads) * head_dim, head_dim), head_dim)
+
+    def scores_of(n, out):
+        r, rows, cols = spot(n)
+        out[...] = lax.dot_general(
+            has["q"][rows, cols], every[KEY][r], (((1,), (1,)), ((), ())), preferred_element_type=jnp.float32
+        )
+
+    def weights_from(n, scores, out):
+        r, _, _ = spot(n)
+        docs = jnp.where(place_of < count_ref[me * REQ_DEV + r] * doc_len, scores[:, :context], very_low)
+        own = jnp.where(causal, scores[:, context:], very_low)
+        top = jnp.maximum(jnp.max(docs, axis=1, keepdims=True), jnp.max(own, axis=1, keepdims=True))
+        out[:, :context] = jnp.exp2((docs - top) * (scale * LOG2E)).astype(jnp.bfloat16)
+        out[:, context:] = jnp.exp2((own - top) * (scale * LOG2E)).astype(jnp.bfloat16)
+
+    def output_of(n, weights):
+        r, rows, cols = spot(n)
+        summed = jnp.dot(weights[...], every[VALUE][r], preferred_element_type=jnp.float32)
+        att_ref[rows, cols] = (summed[:, :head_dim] / summed[:, head_dim:]).astype(jnp.bfloat16)
+
+    score_a, score_b, weight_a, weight_b = (has[n] for n in ("score0", "score1", "weight0", "weight1"))
+    early = [has["early%d" % n] for n in range(EARLY)]
+
+    def early_head(n):
+        if n == 0:
+            fetch[2].wait()
+        scores_of(n, score_a)
+        weights_from(n, score_a, early[n])
+
+    def pair(m, carry):
+        scores_of(2 * m + 1, score_b)
+        weights_from(2 * m, score_a, weight_a)
+        output_of(2 * m - 1, weight_b)
+        scores_of(2 * m + 2, score_a)
+        weights_from(2 * m + 1, score_b, weight_b)
+        output_of(2 * m, weight_a)
+        return carry
+
     begin(KEY)
     for way in range(2):
         ring_of_pos(way, 1).start()
-    pick(KEY, base[KEY], 0)
+    pick(KEY, 0)
     tasks = [lambda: arrive(KEY), lambda: settle(KEY)]
     tasks += [functools.partial(lay_out, KEY, r) for r in range(REQ_DEV)]
     tasks += [functools.partial(key_update, r, g) for r in range(REQ_DEV) for g in range(GROUPS)]
+    tasks += [functools.partial(early_head, n) for n in range(EARLY)]
     lead = min(LEAD, full)
     for tick in range(1, full + lead + 1):
         if tick <= full:
@@ -332,7 +400,7 @@
         if tick == lead:
             fetch[VALUE].wait()
             begin(VALUE)
-            pick(VALUE, base[VALUE], 0)
+            pick(VALUE, 0)
         if tick > lead:
             todo = []
             if tick > full:
@@ -345,6 +413,11 @@
                 ]
             hop(VALUE, tick - lead, todo)
 
+    if nh > 1:
+        other = has["other"]
+        twin = head_at + 1 - 2 * lax.rem(head_at, 2)
+        pl.semaphore_signal(other, inc=1, device_id={"heads": twin}, device_id_type=MESH)
+        pl.semaphore_wait(other, 1)
     give_back(KEY)
     arrive(VALUE)
     settle(VALUE)
@@ -359,54 +432,19 @@
         share(k).start()
     parts[head_at] = squares[...]
 
-    fetch[2].wait()
-    row = lax.broadcasted_iota(jnp.int32, (tokens, span - context), 0)
-    col = lax.broadcasted_iota(jnp.int32, (tokens, span - context), 1)
-    causal = row >= col
-    place_of = lax.broadcasted_iota(jnp.int32, (1, context), 1)
-
-    def spot(n):
-        n = jnp.clip(n, 0, REQ_DEV * heads - 1)
-        r = n // heads
-        rows = pl.ds(pl.multiple_of(r * tokens, 16), tokens)
-        return r, rows, pl.ds(pl.multiple_of(lax.rem(n, heads) * head_dim, head_dim), head_dim)
-
-    def scores_of(n, out):
-        r, rows, cols = spot(n)
-        out[...] = lax.dot_general(
-            has["q"][rows, cols], every[KEY][r], (((1,), (1,)), ((), ())), preferred_element_type=jnp.float32
-        )
-
-    def weights_from(n, scores, out):
-        r, _, _ = spot(n)
-        docs = jnp.where(place_of < count_ref[me * REQ_DEV + r] * doc_len, scores[:, :context], very_low)
-        own = jnp.where(causal, scores[:, context:], very_low)
-        top = jnp.maximum(jnp.max(docs, axis=1, keepdims=True), jnp.max(own, axis=1, keepdims=True))
-        out[:, :context] = jnp.exp2((docs - top) * (scale * LOG2E)).astype(jnp.bfloat16)
-        out[:, context:] = jnp.exp2((own - top) * (scale * LOG2E)).astype(jnp.bfloat16)
-
-    def output_of(n, weights):
-        r, rows, cols = spot(n)
-        summed = jnp.dot(weights[...], every[VALUE][r], preferred_element_type=jnp.float32)
-        att_ref[rows, cols] = (summed[:, :head_dim] / summed[:, head_dim:]).astype(jnp.bfloat16)
-
-    score_a, score_b, weight_a, weight_b = (has[n] for n in ("score0", "score1", "weight0", "weight1"))
-
-    def pair(m, carry):
-        scores_of(2 * m + 1, score_b)
-        weights_from(2 * m, score_a, weight_a)
-        output_of(2 * m - 1, weight_b)
-        scores_of(2 * m + 2, score_a)
-        weights_from(2 * m + 1, score_b, weight_b)
-        output_of(2 * m, weight_a)
-        return carry
-
     weight_b[...] = jnp.ones_like(weight_b)
-    scores_of(0, score_a)
-    lax.fori_loop(0, 1, pair, 0)
+    scores_of(EARLY, score_a)
+    for n in range(EARLY):
+        output_of(n, early[n])
     turn(VALUE)
-    lax.fori_loop(1, REQ_DEV * heads // 2, pair, 0)
+    pairs = REQ_DEV * heads // 2
+    lax.fori_loop(EARLY // 2, EARLY // 2 + 1, pair, 0)
+    output_of(EARLY - 1, early[EARLY - 1])
+    lax.fori_loop(EARLY // 2 + 1, pairs - 2, pair, 0)
+    spread_all(KEY)
+    lax.fori_loop(pairs - 2, pairs, pair, 0)
     output_of(REQ_DEV * heads - 1, weight_b)
+    spread_all(VALUE)
 
     for k in range(1, nh):
         share(k).wait()
@@ -422,9 +460,9 @@
                     ring(p, way, step, chunk).wait_send()
         for t in range(ny):
             last_hop(p, t).wait_send()
-        for j in range(NZ):
+        for step in range(half + 1):
             for t in range(1, ny):
-                across(p, t, j).wait_send()
+                across(p, t, step).wait_send()
     for way in range(2):
         for step in range(1, half + 1 - way):
             ring_of_pos(way, step).wait_send()
@@ -433,16 +471,16 @@
 
     for p in range(2):
 
-        def land(i, carry):
-            back(p, far_first(i)).wait()
+        def leave(i, carry):
+            back(p, far_first(i)).wait_send()
             return carry
 
-        lax.fori_loop(0, ny * (NZ - 2), land, 0)
-        for t in range(ny):
-            if t:
-                back(p, t * NZ).wait()
-            turn_aside(p, t).wait_send()
-            turn_forward(p, t).wait()
+        lax.fori_loop(0, NZ - 2, leave, 0)
+        for w in range(2):
+            turn_aside(p, w).wait_send()
+            turn_forward(p, w).wait_send()
+        for u in range(1, ny):
+            spread(p, u).wait()
 
 
 def blend(slots, table, lists, counts, cache, pos, gain, queries, own):
@@ -469,11 +507,12 @@
             ("far", (ny,) + doc),
             ("last", (ny,) + doc),
             ("picked", (ny, NZ) + doc),
-            ("ctx", (peers,) + doc),
+            ("ctx", (ny, NZ) + doc),
             ("all", (REQ_DEV, span, head_dim * (1 + p))),
             ("fresh", (entries + 1,) + packet),
-            ("upd", (peers,) + packet),
-            ("turn", (ny,) + packet),
+            ("upd", (NZ, ny) + packet),
+            ("turn", (2, ny // 2) + packet),
+            ("mid", (ny, NZ) + packet),
         ):
             scratch["%s%d" % (name, p)] = VMEM(shape, bf16)
         for way in range(2):
@@ -484,6 +523,8 @@
     for name in ("0", "1"):
         scratch["score" + name] = VMEM((tokens, span), f32)
         scratch["weight" + name] = VMEM((tokens, span), bf16)
+    for n in range(EARLY):
+        scratch["early%d" % n] = VMEM((tokens, span), bf16)
     scratch["q"] = VMEM(queries.shape, bf16)
     scratch["own"] = VMEM(own.shape, bf16)
     scratch["dev"] = VMEM((2, entries * dev_tok, head_dim), f32)
@@ -497,13 +538,14 @@
         ("zsend", (2, 2, full, CHUNKS)), ("zrecv", (2, 2, full, CHUNKS)),
         ("lsend", (2, ny)), ("lrecv", (2, ny)),
         ("psend", (2, half + ny)), ("precv", (2, half + ny)),
-        ("ysend", (2, ny, NZ)), ("yrecv", (2, ny, NZ)),
-        ("send", (2, peers)), ("recv", (2, peers)),
-        ("tsend", (2, ny)), ("trecv", (2, ny)),
+        ("ysend", (2, ny, half + 1)), ("yrecv", (2, ny, half + 1)),
+        ("send", (2, NZ + 2)), ("recv", (2, NZ + 2)),
+        ("tsend", (2, 2)), ("trecv", (2, 2)), ("gsend", (2, ny)), ("grecv", (2, ny)),
         ("hsend", (nh,)), ("hrecv", (nh,)),
         ("local_sem", (4,)),
     ):
         scratch[name] = DMA(shape)
+    scratch["other"] = pltpu.SemaphoreType.REGULAR
     any_space, vmem = whole(pl.ANY), whole(VMEM)
     return pl.pallas_call(
         functools.partial(blend_kernel, ny, nh, slots, dev_tok, tuple(scratch)),

time: 148 us -> 144 us (0.973)
  the two profiles are of different devices: /device:TPU:24 before, /device:TPU:6 now
where the time goes in v6:
time: 144 us; the launch traced here: 143 us
  Pallas kernels  136 us (94%)
  local copies, waits for them, and re-layouts  4.39 us (3%)
  other arithmetic  1.73 us (1%)
    pallas_call x1, Pallas kernels, blend(): pl.pallas_call(functools.partial(blend_kernel, ny, nh, slots, dev_tok, tu...  136 us
    unnamed x5, local copies, waits for them, and re-layouts  3.64 us

profile of v6, /device:TPU:6, one launch (start us, length us, event | category | flops | bytes accessed | tf_op | source)
XLA Modules:
  0.0 143.2 jit_solution(12032523544726912231)
XLA Ops:
  0.7 0.7 multiply_add_fusion
  1.4 1.0 select_reduce_fusion.table_ref
  2.4 136.4 %blend.1 = (bf16[384,1024]{1,0:T(8,128)(2,1)}, bf16[64,24,256]{2,1,0:T(8,128)(2,1)}, f32[8,128]{1,0:T(8,128)}) custom-call(s32[256]{0:T(256)} %select_reduce_fusion.table_ref, s32[20,128]{1,0:T(8,128)} %bitcast.7, s32[128]{0:T(128)} %count_ref.1, bf16[6,128,256]{2,1,0:T(8,128)(2,1)} %bitcast.6, s32[6,24]{1,0:T(8,128)} %pos_ref.1, f32[1,256]{1,0:T(1,128)} %gain_ref.1, ...), custom_call_target="tpu_custom_call" | custom-call | tf_op jit(solution)/shard_map/blend/pallas_call | solution.py:550
  138.8 0.8 reshape.144
  139.5 0.6 copy.11
  140.2 0.0 copy-start
  140.2 2.1 %copy.14 = bf16[384,1024]{1,0:T(8,128)(2,1)} copy(bf16[384,1024]{1,0:T(8,128)(2,1)} %get-tuple-element.26) | data formatting | bytes 1572864
  142.3 0.0 copy-done
  142.3 0.9 copy.15
  (4 shorter events, 0.0 us)
Async XLA Ops:
  140.2 2.1 %copy-start = (bf16[64,24,256]{2,1,0:T(8,128)(2,1)S(1)}, bf16[64,24,256]{2,1,0:T(8,128)(2,1)}, u32[]{:S(2)}) copy-start(bf16[64,24,256]{2,1,0:T(8,128)(2,1)} %get-tuple-element.27) | copy-start | bytes 2359300

commit v7 on v6

--- a/solution.py
+++ b/solution.py
@@ -18,9 +18,9 @@
 MESH = pl.DeviceIdType.MESH
 LOG2E = 1.4426950408889634
 GROUPS = 4
-LEAD = 4
+LEAD = 6
 CHUNKS = 2
-EARLY = 4
+EARLY = 2
 KEY, VALUE = 0, 1
 
 
@@ -392,7 +392,6 @@
     tasks = [lambda: arrive(KEY), lambda: settle(KEY)]
     tasks += [functools.partial(lay_out, KEY, r) for r in range(REQ_DEV)]
     tasks += [functools.partial(key_update, r, g) for r in range(REQ_DEV) for g in range(GROUPS)]
-    tasks += [functools.partial(early_head, n) for n in range(EARLY)]
     lead = min(LEAD, full)
     for tick in range(1, full + lead + 1):
         if tick <= full:
@@ -402,16 +401,19 @@
             begin(VALUE)
             pick(VALUE, 0)
         if tick > lead:
+            since = tick - full
+            counts = (0, 1 if since in (2, 3) else 0)
+            if since > 3:
+                each_slot = -(-len(tasks) // (2 * (lead + 1 - since)))
+                counts = (each_slot, each_slot)
             todo = []
-            if tick > full:
-                share_of = -(-len(tasks) // (full + lead + 1 - tick))
-                turns, tasks = tasks[:share_of], tasks[share_of:]
-                middle = len(turns) // 2
-                todo = [
-                    functools.partial(lambda some: [one() for one in some], turns[:middle]),
-                    functools.partial(lambda some: [one() for one in some], turns[middle:]),
-                ]
+            for some in counts:
+                turns, tasks = tasks[:some], tasks[some:]
+                todo.append(functools.partial(lambda turns: [one() for one in turns], turns))
             hop(VALUE, tick - lead, todo)
+
+    for task in tasks:
+        task()
 
     if nh > 1:
         other = has["other"]
@@ -419,7 +421,10 @@
         pl.semaphore_signal(other, inc=1, device_id={"heads": twin}, device_id_type=MESH)
         pl.semaphore_wait(other, 1)
     give_back(KEY)
+    early_head(0)
     arrive(VALUE)
+    for n in range(1, EARLY):
+        early_head(n)
     settle(VALUE)
     turn(KEY)
     for r in range(REQ_DEV):

time: 144 us -> 143 us (level)
    pallas_call x1, Pallas kernels: 136 us -> 135 us  [blend(): pl.pallas_call(functools.partial(blend_kernel, ny, nh, slots, dev_tok, tu...]
where the time goes in v7:
time: 143 us; the launch traced here: 142 us
  Pallas kernels  135 us (94%)
  local copies, waits for them, and re-layouts  4.39 us (3%)
  other arithmetic  1.73 us (1%)
    pallas_call x1, Pallas kernels, blend(): pl.pallas_call(functools.partial(blend_kernel, ny, nh, slots, dev_tok, tu...  135 us
    unnamed x5, local copies, waits for them, and re-layouts  3.64 us

profile of v7, /device:TPU:6, one launch (start us, length us, event | category | flops | bytes accessed | tf_op | source)
XLA Modules:
  0.0 141.7 jit_solution(12523051558287195847)
XLA Ops:
  0.7 0.7 multiply_add_fusion
  1.4 1.0 select_reduce_fusion.table_ref
  2.4 134.9 %blend.1 = (bf16[384,1024]{1,0:T(8,128)(2,1)}, bf16[64,24,256]{2,1,0:T(8,128)(2,1)}, f32[8,128]{1,0:T(8,128)}) custom-call(s32[256]{0:T(256)} %select_reduce_fusion.table_ref, s32[20,128]{1,0:T(8,128)} %bitcast.7, s32[128]{0:T(128)} %count_ref.1, bf16[6,128,256]{2,1,0:T(8,128)(2,1)} %bitcast.6, s32[6,24]{1,0:T(8,128)} %pos_ref.1, f32[1,256]{1,0:T(1,128)} %gain_ref.1, ...), custom_call_target="tpu_custom_call" | custom-call | tf_op jit(solution)/shard_map/blend/pallas_call | solution.py:555
  137.3 0.8 reshape.144
  138.1 0.6 copy.11
  138.7 0.0 copy-start
  138.7 2.1 %copy.14 = bf16[384,1024]{1,0:T(8,128)(2,1)} copy(bf16[384,1024]{1,0:T(8,128)(2,1)} %get-tuple-element.26) | data formatting | bytes 1572864
  140.8 0.0 copy-done
  140.8 0.9 copy.15
  (4 shorter events, 0.0 us)
Async XLA Ops:
  138.7 2.1 %copy-start = (bf16[64,24,256]{2,1,0:T(8,128)(2,1)S(1)}, bf16[64,24,256]{2,1,0:T(8,128)(2,1)}, u32[]{:S(2)}) copy-start(bf16[64,24,256]{2,1,0:T(8,128)(2,1)} %get-tuple-element.27) | copy-start | bytes 2359300

commit v8 on v7

--- a/solution.py
+++ b/solution.py
@@ -58,8 +58,8 @@
     def two(name):
         return has[name + "0"], has[name + "1"]
 
-    base, far, last_pick, picked, ctx, every, fresh, upd, turn_buf, mid = map(
-        two, ("base", "far", "last", "picked", "ctx", "all", "fresh", "upd", "turn", "mid")
+    base, far, last_pick, picked, relay, ctx, every, fresh, upd, turn_buf, mid = map(
+        two, ("base", "far", "last", "picked", "relay", "ctx", "all", "fresh", "upd", "turn", "mid")
     )
     passing = [[[has["ring%d%d%d" % (p, way, s)] for s in range(full)] for way in range(2)] for p in range(2)]
     ring_pos, all_pos, dev, squares, parts = (has[n] for n in ("ring_pos", "all_pos", "dev", "squares", "parts"))
@@ -128,8 +128,23 @@
     def across(p, t, step):
         at = pl.ds(1 if step == half else 2 * step, 1 if step in (0, half) else 2)
         src = far[p].at[pl.ds(t, 1)] if step == half else picked[p].at[t, at]
+        if relayed(t, step):
+            sems = has["ysend"].at[p, t, step], has["frecv"].at[p, step // 2]
+            return remote(src, relay[p].at[step // 2], *sems, along_y[ny - 1])
         sems = has["ysend"].at[p, t, step], has["yrecv"].at[p, t, step]
         return remote(src, ctx[p].at[t, at], *sems, along_y[t])
+
+    def relayed(t, step):
+        return 2 * t == ny > 2 and step < half and step % 2 == 1
+
+    def forward(p, step):
+        sems = has["fsend"].at[p, step // 2], has["yrecv"].at[p, ny // 2, step]
+        return remote(relay[p].at[step // 2], ctx[p].at[ny // 2, pl.ds(2 * step, 2)], *sems, along_y[ny - 1])
+
+    def pass_on(p, step):
+        if step > 0 and relayed(ny // 2, step):
+            across(p, ny // 2, step).wait_recv()
+            forward(p, step).start()
 
     def pick(p, step):
         for t in list(range(1, ny)) + [0]:
@@ -168,12 +183,15 @@
                 last_pick[p][t] = buf[lax.rem(table_ref[2 * peers + t], 8)]
                 last_hop(p, t).start()
         pick(p, step)
+        pass_on(p, step - 2)
         if todo:
             todo.pop(0)()
 
     def arrive(p):
         for t in range(ny):
             last_hop(p, t).wait_recv()
+        pass_on(p, full - 1)
+        pass_on(p, full)
         for t in range(1, ny):
             across(p, t, half).start()
         ctx[p][0, 1] = far[p][0]
@@ -196,7 +214,7 @@
     def settle(p):
         for step in range(half + 1):
             for t in range(1, ny):
-                across(p, t, step).wait_recv()
+                (forward(p, step) if relayed(t, step) else across(p, t, step)).wait_recv()
         if p == KEY:
             for t in range(1, ny):
                 pos_across(t).wait_recv()
@@ -468,6 +486,8 @@
         for step in range(half + 1):
             for t in range(1, ny):
                 across(p, t, step).wait_send()
+                if relayed(t, step):
+                    forward(p, step).wait_send()
     for way in range(2):
         for step in range(1, half + 1 - way):
             ring_of_pos(way, step).wait_send()
@@ -512,6 +532,7 @@
             ("far", (ny,) + doc),
             ("last", (ny,) + doc),
             ("picked", (ny, NZ) + doc),
+            ("relay", (half // 2, 2) + doc),
             ("ctx", (ny, NZ) + doc),
             ("all", (REQ_DEV, span, head_dim * (1 + p))),
             ("fresh", (entries + 1,) + packet),
@@ -544,6 +565,7 @@
         ("lsend", (2, ny)), ("lrecv", (2, ny)),
         ("psend", (2, half + ny)), ("precv", (2, half + ny)),
         ("ysend", (2, ny, half + 1)), ("yrecv", (2, ny, half + 1)),
+        ("fsend", (2, half // 2)), ("frecv", (2, half // 2)),
         ("send", (2, NZ + 2)), ("recv", (2, NZ + 2)),
         ("tsend", (2, 2)), ("trecv", (2, 2)), ("gsend", (2, ny)), ("grecv", (2, ny)),
         ("hsend", (nh,)), ("hrecv", (nh,)),

time: 143 us -> 149 us (1.042)
  Pallas kernels: 135 us -> 141 us
    pallas_call x1, Pallas kernels: 135 us -> 141 us  [blend(): pl.pallas_call(functools.partial(blend_kernel, ny, nh, slots, dev_tok, tu...]
where the time goes in v8:
time: 149 us; the launch traced here: 148 us
  Pallas kernels  141 us (95%)
  local copies, waits for them, and re-layouts  4.39 us (3%)
  other arithmetic  1.73 us (1%)
    pallas_call x1, Pallas kernels, blend(): pl.pallas_call(functools.partial(blend_kernel, ny, nh, slots, dev_tok, tu...  141 us
    unnamed x5, local copies, waits for them, and re-layouts  3.64 us

profile of v8, /device:TPU:6, one launch (start us, length us, event | category | flops | bytes accessed | tf_op | source)
XLA Modules:
  0.0 148.3 jit_solution(7554725128166726596)
XLA Ops:
  0.7 0.7 multiply_add_fusion
  1.4 1.0 select_reduce_fusion.table_ref
  2.4 141.5 %blend.1 = (bf16[384,1024]{1,0:T(8,128)(2,1)}, bf16[64,24,256]{2,1,0:T(8,128)(2,1)}, f32[8,128]{1,0:T(8,128)}) custom-call(s32[256]{0:T(256)} %select_reduce_fusion.table_ref, s32[20,128]{1,0:T(8,128)} %bitcast.7, s32[128]{0:T(128)} %count_ref.1, bf16[6,128,256]{2,1,0:T(8,128)(2,1)} %bitcast.6, s32[6,24]{1,0:T(8,128)} %pos_ref.1, f32[1,256]{1,0:T(1,128)} %gain_ref.1, ...), custom_call_target="tpu_custom_call" | custom-call | tf_op jit(solution)/shard_map/blend/pallas_call | solution.py:577
  143.9 0.8 reshape.144
  144.7 0.6 copy.11
  145.3 0.0 copy-start
  145.3 2.1 %copy.14 = bf16[384,1024]{1,0:T(8,128)(2,1)} copy(bf16[384,1024]{1,0:T(8,128)(2,1)} %get-tuple-element.26) | data formatting | bytes 1572864
  147.4 0.0 copy-done
  147.4 0.9 copy.15
  (4 shorter events, 0.0 us)
Async XLA Ops:
  145.3 2.1 %copy-start = (bf16[64,24,256]{2,1,0:T(8,128)(2,1)S(1)}, bf16[64,24,256]{2,1,0:T(8,128)(2,1)}, u32[]{:S(2)}) copy-start(bf16[64,24,256]{2,1,0:T(8,128)(2,1)} %get-tuple-element.27) | copy-start | bytes 2359300
